TPU v7x, 32 devices: a whole 2x2x4 slice. The times are simulated.
32 devices in a mesh: dp: 4 (over y, core), fsdp: 8 (over z, x).
Axes of the slice: x: 2, y: 2, z: 4, core: 2. Of those that a mesh axis runs over, the one named last changes fastest.
Arguments:
- char_codes: int32 [32, 128, 16], P(('dp', 'fsdp')), may hold values from 0 to 255
- char_counts: int32 [32, 128], P(('dp', 'fsdp')), may hold values from 1 to 16, as said below
- word_groups: int32 [32, 128], P(('dp', 'fsdp')), may hold values from 0 to 7
- valid_words: int32 [32], P(('dp', 'fsdp')), may hold values from 16 to 128, as said below
- char_matrix: bfloat16 [8192, 128], P(('dp', 'fsdp'))
- char_lookup: bfloat16 [256, 256], P(('dp', 'fsdp')), may hold values from -6 to 6
- group_lookup: bfloat16 [256, 8], P(('dp', 'fsdp')), may hold values from -6 to 6
- char_vectors: bfloat16 [256, 5], P(('dp', 'fsdp'))
- word_matrix: bfloat16 [24576, 128], P(('dp', 'fsdp'))
- word_vectors: bfloat16 [512, 4], P(('dp', 'fsdp'))
- cotangent: bfloat16 [32, 128, 512], P(('dp', 'fsdp')), may hold values from -6 to 6
Outputs:
- layer_out: bfloat16 [32, 128, 512], P(('dp', 'fsdp'))
- grad_char_matrix: float32 [8192, 128], P(('dp', 'fsdp'))
- grad_char_lookup: float32 [256, 256], P(('dp', 'fsdp'))
- grad_group_lookup: float32 [256, 8], P(('dp', 'fsdp'))
- grad_char_vectors: float32 [256, 5], P(('dp', 'fsdp'))
- grad_word_matrix: float32 [24576, 128], P(('dp', 'fsdp'))
- grad_word_vectors: float32 [512, 4], P(('dp', 'fsdp'))
Inputs may be any that keep to these rules, and one draw needn't show every extreme that they name: `char_counts`: in every sequence some word has all 16 characters. `valid_words`: some sequence has all 128 words real.
All inputs are finite; a program needn't handle non-finite values.
Results may differ from a plain program's by a relative error of at most 0.015.
Values may be sent and summed in bfloat16 or wider, within the bound.
A program may use at most 192 MiB of HBM per device.

v0:
```python
import functools

import jax
import jax.numpy as jnp
from jax import lax
from jax.experimental import pallas as pl
from jax.experimental.pallas import tpu as pltpu
from jax.sharding import PartitionSpec as P

C = 256
HD = 64
CH = 4
CM = 1024
D = 512
H = 8
FF = 2048
W = 16
VOCAB = 256
LANGS = 8
LEN = 128
C_COLS = 6 * C + 2 * CM + D
D_COLS = 4 * D + 2 * FF
EPSILON = 1e-05
NEGATIVE = -1000000000.0
F32 = jnp.float32
BF16 = jnp.bfloat16
FWD_ROWS = 256
BWD_ROWS = 256
STAGE = 0
VMEM_LIMIT = 63 << 20

MESH = pl.DeviceIdType.MESH


class Grid:
    def __init__(self, sizes):
        self.Y, self.Z, self.X = sizes
        dp, fs = lax.axis_index("dp"), lax.axis_index("fsdp")
        self.y, self.c = dp // 2, dp % 2
        self.z, self.x = fs // self.X, fs % self.X

    def at(self, y=None, c=None, z=None, x=None):
        y = self.y if y is None else y
        c = self.c if c is None else c
        z = self.z if z is None else z
        x = self.x if x is None else x
        return (y * 2 + c, z * self.X + x)

    def others(self, axis):
        n, me = {"y": (self.Y, self.y), "z": (self.Z, self.z), "x": (self.X, self.x)}[axis]
        return [(me + k) % n for k in range(1, n)]

    def partners(self):
        out = [self.at(c=1 - self.c)]
        for axis in "yzx":
            out += [self.at(**{axis: v}) for v in self.others(axis)]
        return out

    def greet(self):
        barrier = pltpu.get_barrier_semaphore()
        all_of = self.partners()
        for p in all_of:
            pl.semaphore_signal(barrier, inc=1, device_id=p, device_id_type=MESH)
        pl.semaphore_wait(barrier, len(all_of))


class Sems:
    def __init__(self, send, recv):
        self.send, self.recv, self.n = send, recv, 0

    def copy(self, src, dst, to):
        i = self.n
        self.n += 1
        d = pltpu.make_async_remote_copy(
            src_ref=src, dst_ref=dst, send_sem=self.send.at[i], recv_sem=self.recv.at[i],
            device_id=to, device_id_type=MESH)
        d.start()
        return d


def ag_count(Y, Z, X):
    return (Z - 1) + 1 + 2 * ((X - 1) + (Y - 1)) + 2 * ((X - 1) + (Y - 1))


class Gather:
    def __init__(self, grid, src, G, sems, half):
        self.g, self.src, self.G, self.s, self.half = grid, src, G, sems, half
        self.sent = []
        self.core = []

    def send(self, idx, to, keep):
        d = self.s.copy(self.G.at[idx], self.G.at[idx], to)
        self.sent.append(d)
        keep.append(d)

    def start(self):
        g = self.g
        self.p1 = []
        for z in g.others("z"):
            d = self.s.copy(self.src, self.G.at[g.y, g.c, g.z, g.x], g.at(z=z))
            self.sent.append(d)
            self.p1.append(d)

    def step2(self):
        g, h = self.g, self.half
        n = self.G.shape[4]
        self.A, self.B = pl.ds(0, h), pl.ds(h, n - h)
        for d in self.p1:
            d.wait_recv()
        self.p2a, self.p2b = [], []
        for x in g.others("x"):
            self.send((g.y, g.c, slice(None), g.x, self.A), g.at(x=x), self.p2a)
        for y in g.others("y"):
            self.send((g.y, g.c, slice(None), g.x, self.B), g.at(y=y), self.p2b)
        self.send((g.y, g.c, slice(None), g.x), g.at(c=1 - g.c), self.core)

    def step3(self):
        g = self.g
        self.p3a, self.p3b = [], []
        for d in self.p2a:
            d.wait_recv()
        for y in g.others("y"):
            self.send((g.y, g.c, slice(None), slice(None), self.A), g.at(y=y), self.p3a)
        for d in self.p2b:
            d.wait_recv()
        for x in g.others("x"):
            self.send((slice(None), g.c, slice(None), g.x, self.B), g.at(x=x), self.p3b)
        for x in g.others("x"):
            self.send((g.y, g.c, slice(None), x, self.A), g.at(c=1 - g.c), self.core)
        for y in g.others("y"):
            self.send((y, g.c, slice(None), g.x, self.B), g.at(c=1 - g.c), self.core)

    def step4(self):
        g = self.g
        for d in self.p3a:
            d.wait_recv()
        for y in g.others("y"):
            self.send((y, g.c, slice(None), slice(None), self.A), g.at(c=1 - g.c), self.core)
        for d in self.p3b:
            d.wait_recv()
        for x in g.others("x"):
            self.send((slice(None), g.c, slice(None), x, self.B), g.at(c=1 - g.c), self.core)

    def finish(self):
        for d in self.core:
            d.wait_recv()

    def drain(self):
        for d in self.sent:
            d.wait_send()


def rs_count(Y, Z, X):
    return 1 + 2 * ((X - 1) + (Y - 1)) + 2 * (Z - 1)


def rs_scratch(Y, Z, X, R, half):
    hb = R - half
    b = jnp.bfloat16
    return [
        pltpu.VMEM((Y, Z, X, R, 128), b),
        pltpu.VMEM((Y - 1, Z, X, half, 128), b),
        pltpu.VMEM((X - 1, Z, half, 128), b),
        pltpu.VMEM((X - 1, Y, Z, hb, 128), b),
        pltpu.VMEM((Y - 1, Z, hb, 128), b),
        pltpu.VMEM((Z - 1, R, 128), b),
    ]


def add_into(dst, srcs):
    lead = dst.shape[:-2]
    total = 1
    for n in lead:
        total *= n

    def body(i, _):
        idx, r = [], i
        for n in reversed(lead):
            idx.append(r % n)
            r = r // n
        idx = tuple(reversed(idx))
        acc = dst[idx].astype(jnp.float32)
        for s in srcs:
            acc = acc + s[idx].astype(jnp.float32)
        dst[idx] = acc.astype(jnp.bfloat16)
        return 0

    lax.fori_loop(0, total, body, 0)


class Scatter:
    def __init__(self, grid, PB, recv, sems, half):
        self.g, self.PB, self.s, self.half = grid, PB, sems, half
        self.r1, self.r2a, self.r3a, self.r2b, self.r3b, self.r4 = recv
        self.sent = []

    def send(self, src, dst, to, keep):
        d = self.s.copy(src, dst, to)
        self.sent.append(d)
        keep.append(d)

    def start(self):
        g = self.g
        self.p1 = []
        self.send(self.PB.at[:, 1 - g.c], self.r1, g.at(c=1 - g.c), self.p1)


    def step2(self):
        g, h = self.g, self.half
        n = self.PB.shape[4]
        self.A, self.B = pl.ds(0, h), pl.ds(h, n - h)
        for d in self.p1:
            d.wait_recv()
        add_into(self.PB.at[:, g.c], [self.r1])
        self.p2a, self.p2b = [], []
        for k, y in enumerate(g.others("y")):
            self.send(self.PB.at[y, g.c, :, :, self.A], self.r2a.at[k], g.at(y=y), self.p2a)
        for k, x in enumerate(g.others("x")):
            self.send(self.PB.at[:, g.c, :, x, self.B], self.r2b.at[k], g.at(x=x), self.p2b)

    def step3(self):
        g = self.g
        self.p3a, self.p3b = [], []
        for d in self.p2a:
            d.wait_recv()
        add_into(self.PB.at[g.y, g.c, :, :, self.A], [self.r2a.at[k] for k in range(g.Y - 1)])
        for k, x in enumerate(g.others("x")):
            self.send(self.PB.at[g.y, g.c, :, x, self.A], self.r3a.at[k], g.at(x=x), self.p3a)
        for d in self.p2b:
            d.wait_recv()
        add_into(self.PB.at[:, g.c, :, g.x, self.B], [self.r2b.at[k] for k in range(g.X - 1)])
        for k, y in enumerate(g.others("y")):
            self.send(self.PB.at[y, g.c, :, g.x, self.B], self.r3b.at[k], g.at(y=y), self.p3b)

    def step4(self):
        g = self.g
        self.p4 = []
        for part, waits, recv in ((self.A, self.p3a, self.r3a), (self.B, self.p3b, self.r3b)):
            for d in waits:
                d.wait_recv()
            add_into(self.PB.at[g.y, g.c, :, g.x, part], [recv.at[k] for k in range(recv.shape[0])])
            for k, z in enumerate(g.others("z")):
                self.send(self.PB.at[g.y, g.c, z, g.x, part], self.r4.at[k, part], g.at(z=z), self.p4)

    def finish(self, place, rows, count):
        g = self.g
        for d in self.p4:
            d.wait_recv()
        unit = max(1, 16 // rows)
        for t in range(-(-count // unit)):
            r = slice(t * unit * rows, (t + 1) * unit * rows)
            acc = self.PB[g.y, g.c, g.z, g.x, r].astype(jnp.float32)
            for k in range(g.Z - 1):
                acc = acc + self.r4[k, r].astype(jnp.float32)
            for u in range(unit):
                if t * unit + u < count:
                    place(t * unit + u, acc[u * rows : (u + 1) * rows])

    def drain(self):
        for d in self.sent:
            d.wait_send()


def dot(a, b):
    return lax.dot_general(a, b, (((1,), (0,)), ((), ())), preferred_element_type=F32)


def dot_nt(a, b):
    return lax.dot_general(a, b, (((1,), (1,)), ((), ())), preferred_element_type=F32)


def dot_tn(a, b):
    return lax.dot_general(a, b, (((0,), (0,)), ((), ())), preferred_element_type=F32)


def low(v):
    return v.astype(BF16)


def norm_stats(x):
    centre = x - jnp.mean(x, -1, keepdims=True)
    spread = jnp.mean(centre * centre, -1, keepdims=True)
    scale = lax.rsqrt(spread + EPSILON)
    return centre * scale, scale


def norm_back(grad, xhat, scale, gain):
    inner = grad * gain
    first = jnp.mean(inner, -1, keepdims=True)
    second = jnp.mean(inner * xhat, -1, keepdims=True)
    return scale * (inner - first - xhat * second)


def gelu_both(z):
    sq = z * z
    t = jnp.tanh(z * (0.7978845608028654 + (0.7978845608028654 * 0.044715) * sq))
    h = 0.5 * z
    value = h + h * t
    slope = 0.5 + 0.5 * t + h * (1.0 - t * t) * (
        0.7978845608028654 + (3.0 * 0.7978845608028654 * 0.044715) * sq
    )
    return value, slope


def iota(shape, dim):
    return lax.broadcasted_iota(jnp.int32, shape, dim)


def head_rows(dtype):
    lane = iota((1, 128), 1)
    return [(lane // HD == h).astype(F32).astype(dtype) for h in range(2)]


def head_stack(block, heads):
    return jnp.concatenate([block * h for h in heads], 0)


def own_word(scores, lane_word):
    split = scores.reshape(2, 8, W, 128)
    out = split[:, 0]
    for w in range(1, 8):
        out = jnp.where(lane_word == w, split[:, w], out)
    return out


def spread_words(compact, word_rows):
    return jnp.concatenate([compact[h] * word_rows[w] for h in range(2) for w in range(8)], 0)


def side_by_side(stacked, rows):
    return jnp.concatenate([stacked[h * rows : (h + 1) * rows] for h in range(2)], 1)


def place_own(own, raw, staged, extra, rows, blocks, total):
    staged[...] = raw[...].astype(F32)
    unit = max(1, 16 // rows)

    def block(j):
        if j < blocks:
            if rows == 1:
                return staged[j : j + 1, :]
            return staged[pl.ds(j, rows, stride=blocks), :]
        at = (j - blocks) * 128
        if at < extra.shape[1]:
            return extra[:, at : at + 128]
        return jnp.zeros((rows, 128), F32)

    for t in range(total // unit):
        tile = jnp.concatenate([block(j) for j in range(t * unit, (t + 1) * unit)], 0)
        own[t * unit * rows : (t + 1) * unit * rows, :] = low(tile)


def assemble(G, Wd, rows, total):
    unit = max(1, 16 // rows)
    devices = Wd.shape[0] // rows
    for t in range(total // unit):
        tile = G[:, :, :, :, t * unit * rows : (t + 1) * unit * rows, :]
        if unit == 1:
            Wd[:, t * 128 : (t + 1) * 128] = tile.reshape(devices * rows, 128)
            continue
        tile = tile.reshape(devices, 16, 128).astype(F32)
        for u in range(unit):
            j = t * unit + u
            Wd[:, j * 128 : (j + 1) * 128] = low(
                tile[:, u * rows : (u + 1) * rows, :].reshape(devices * rows, 128)
            )


def pack_blocks(PB, at, blocks, rows):
    unit = max(1, 16 // rows)
    lead = PB.shape[:4]
    devices = lead[0] * lead[1] * lead[2] * lead[3]
    for t in range(len(blocks) // unit):
        parts = [b.reshape(devices, rows, 128) for b in blocks[t * unit : (t + 1) * unit]]
        tile = low(parts[0] if unit == 1 else jnp.concatenate(parts, 1))
        row = (at + t * unit) * rows
        PB[:, :, :, :, row : row + unit * rows, :] = tile.reshape(lead + (unit * rows, 128))


def columns(value):
    return [value[:, k : k + 128] for k in range(0, value.shape[1], 128)]


class Layout:
    def __init__(self, sizes):
        self.sizes = sizes
        Y, Z, X = sizes
        self.lead = (Y, 2, Z, X)
        self.devices = Y * 2 * Z * X
        self.rc = C // self.devices
        self.rw = D // self.devices
        self.bc = C_COLS // 128
        self.bw = D_COLS // 128

        def padded(n, rows):
            unit = max(1, 16 // rows)
            return max(-(-n // unit), 2) * unit

        self.jc = padded(self.bc + 3, self.rc)
        self.jw = padded(self.bw + 1, self.rw)
        self.j1 = padded(24, self.rc)
        self.j2 = padded(11, self.rc)


def half_of(rows):
    return max(16, rows // 32 * 16)


def mono(
    lay, stage, ints, cm, exc, wm, exw, cot,
    out_y, out_cm, out_lookup, out_group, out_vec, out_wm, out_wvec,
    Gc, Gw, Wc, Wwt, PB1, PB2, PBw, stc, stw,
    xh1, n1s, qkvs, probs, os, xh2, n2s, acts, slopes, r2s, alphas, scales, dr1s,
    Us, Ys, accq, acco, accu, accd, acct, sums, tsum,
    lsem, ssc, rsc, ssw, rsw, ss1, rs1, ss2, rs2, ssx, rsx, *recv,
):
    Y, Z, X = lay.sizes
    g = Grid(lay.sizes)
    me = (g.y, g.c, g.z, g.x)
    on = stage

    ag_c = Gather(g, Gc.at[me], Gc, Sems(ssc, rsc), half_of(Gc.shape[4]))
    ag_w = Gather(g, Gw.at[me], Gw, Sems(ssw, rsw), half_of(Gw.shape[4]))
    place_own(Gc.at[me], cm, stc, exc, lay.rc, lay.bc, lay.jc)
    g.greet()
    ag_c.start()
    place_own(Gw.at[me], wm, stw, exw, lay.rw, lay.bw, lay.jw)
    ag_w.start()
    ag_c.step2()
    ag_c.step3()
    ag_c.step4()
    ag_c.finish()
    assemble(Gc, Wc, lay.rc, lay.jc)

    eye = (iota((16, 128), 0) == iota((16, 128), 1)).astype(F32).astype(BF16)
    rows_c = dot_nt(eye, Wc[:, (lay.bc + 2) * 128 : (lay.bc + 3) * 128])
    gain1, shift1, gain2, shift2 = (rows_c[8 + k : 9 + k] for k in range(4))
    query = rows_c[12:13]
    table_low = low(jnp.where(iota((16, C), 0) < LANGS, rows_c, 0.0))
    lookup = slice(lay.bc * 128, (lay.bc + 2) * 128)
    AQ, AO = slice(0, 3 * C), slice(3 * C, 4 * C)
    AU, AD = slice(4 * C, 4 * C + CM), slice(4 * C + CM, 4 * C + 2 * CM)
    PK, PV = slice(4 * C + 2 * CM, 5 * C + 2 * CM), slice(5 * C + 2 * CM, 6 * C + 2 * CM)
    PR = slice(6 * C + 2 * CM, 6 * C + 2 * CM + D)

    lane = iota((1, 128), 1)
    lane_word = lane // W
    word_rows = [(lane_word == w).astype(F32).astype(BF16) for w in range(8)]
    heads = head_rows(BF16)
    head_of = iota((128, C), 0) % 32 // 8 == iota((128, C), 1) // HD
    pq_rows = jnp.where(head_of, query * 0.125, 0.0)
    score_map = dot_nt(low(pq_rows), Wc[:, PK])
    map_hi = low(score_map)
    map_lo = low(score_map - map_hi.astype(F32))
    key_row = iota((1, W, 1), 1)
    pool_own = iota((128, 128), 0) // W == iota((128, 128), 1) % 8
    pool_slot = iota((128, 128), 0) % W

    def onehots(i, groups):
        parts = []
        for k in range(groups):
            r = i * groups + k
            codes = ints[pl.ds(r, 1), :]
            langs = ints[pl.ds(16 + r, 1), :]
            a = (iota((VOCAB, 128), 0) == codes).astype(F32).astype(BF16)
            b = (iota((16, 128), 0) == langs).astype(F32).astype(BF16)
            parts.append(jnp.concatenate([a, b], 0))
        return parts

    GF = FWD_ROWS // 128

    def forward(i, _):
        rows = pl.ds(pl.multiple_of(i * FWD_ROWS, FWD_ROWS), FWD_ROWS)
        table = jnp.concatenate([Wc[:, lookup], table_low], 0)
        e = jnp.concatenate([dot_tn(h, table) for h in onehots(i, GF)], 0)
        xhat, scale1 = norm_stats(e)
        n1 = low(xhat * gain1 + shift1)
        xh1[rows, :] = low(xhat)
        n1s[rows, :] = n1
        qkv = low(dot(n1, Wc[:, AQ]))
        qkvs[rows, :] = qkv
        mixed = []
        for k in range(GF):
            visible = key_row < ints[pl.ds(32 + i * GF + k, 1), :].reshape(1, 1, 128)
            pair_out = []
            for p in range(2):
                q, kk, v = (
                    qkv[k * 128 : (k + 1) * 128, b * C + p * 128 : b * C + (p + 1) * 128]
                    for b in range(3)
                )
                s = own_word(dot_nt(head_stack(kk, heads), q), lane_word) * 0.125
                s = jnp.where(visible, s, NEGATIVE)
                s = jnp.exp(s - jnp.max(s, 1, keepdims=True))
                prob = s / jnp.sum(s, 1, keepdims=True)
                probs[i * GF + k, 2 * p : 2 * p + 2] = prob
                pair_out.append(dot_tn(spread_words(low(prob), word_rows), head_stack(v, heads)))
            mixed.append(jnp.concatenate(pair_out, 1))
        o = low(jnp.concatenate(mixed, 0))
        os[rows, :] = o
        r1 = e + dot(o, Wc[:, AO])
        xhat, scale2 = norm_stats(r1)
        n2 = low(xhat * gain2 + shift2)
        xh2[rows, :] = low(xhat)
        n2s[rows, :] = n2
        scales[rows, 0:1] = scale1
        scales[rows, 1:2] = scale2
        value, slope = gelu_both(dot(n2, Wc[:, AU]))
        act = low(value)
        acts[rows, :] = act
        slopes[rows, :] = low(slope)
        r2 = low(r1 + dot_nt(act, Wc[:, AD]))
        r2s[rows, :] = r2
        for k in range(GF):
            r = i * GF + k
            own = r2[k * 128 : (k + 1) * 128]
            s = dot_nt(own, map_hi) + dot_nt(own, map_lo)
            seen = pool_own & (pool_slot < ints[pl.ds(48 + r, 1), :])
            s = jnp.where(seen, s, NEGATIVE)
            s = jnp.where(seen, jnp.exp(s - jnp.max(s, 0, keepdims=True)), 0.0)
            alpha = s / jnp.sum(s, 0, keepdims=True)
            alphas[pl.ds(pl.multiple_of(r * 128, 128), 128), :] = alpha
            u = dot_tn(low(alpha)[:, :32], own)
            for h in range(CH):
                Us[h, pl.ds(pl.multiple_of(r * 8, 8), 8), :] = u[8 * h : 8 * h + 8]
        return 0

    nf = LEN * W // FWD_ROWS
    lax.fori_loop(0, nf // 2, forward, 0)
    ag_w.step2()
    ag_w.step3()
    lax.fori_loop(nf // 2, nf, forward, 0)
    ag_w.step4()

    head_c = [iota((1, C), 1) // HD == h for h in range(CH)]
    pooled = sum(jnp.where(head_c[h], dot(low(Us[h]), Wc[:, PV]), 0.0) for h in range(CH))
    pooled_low = low(pooled)
    w_in = dot(pooled_low, Wc[:, PR])

    ag_w.finish()
    if lay.rw >= 16:

        def wcols(lo, hi):
            return jnp.concatenate(
                [
                    Gw[:, :, :, :, j * lay.rw : (j + 1) * lay.rw, :].reshape(D, 128)
                    for j in range(lo // 128, hi // 128)
                ],
                1,
            )

    else:
        assemble(Gw, Wwt, lay.rw, lay.jw)

        def wcols(lo, hi):
            return Wwt[:, lo:hi]

    rows_w = dot_nt(eye, wcols(D_COLS, D_COLS + 128))
    f1, c1, f2, c2 = (rows_w[k : k + 1] for k in range(4))
    BQ, BO, BU, BD = (0, 3 * D), (3 * D, 4 * D), (4 * D, 4 * D + FF), (4 * D + FF, D_COLS)
    NP = H // 2

    xhat1, sc1 = norm_stats(w_in)
    m1 = low(xhat1 * f1 + c1)
    qkv = low(dot(m1, wcols(*BQ)))
    key = iota((1, 128, 1), 1)
    seen_word = (key <= iota((1, 1, 128), 2)) & (key < ints[64:65, :].reshape(1, 1, 128))
    pw, kst, qst, vst, mix = [], [], [], [], []
    for p in range(NP):
        q, kk, v = (qkv[:, b * D + p * 128 : b * D + (p + 1) * 128] for b in range(3))
        kst.append(head_stack(kk, heads))
        qst.append(head_stack(q, heads))
        vst.append(head_stack(v, heads))
        s = dot_nt(kst[p], q).reshape(2, 128, 128) * 0.125
        s = jnp.where(seen_word, s, NEGATIVE)
        s = jnp.exp(s - jnp.max(s, 1, keepdims=True))
        pw.append(s / jnp.sum(s, 1, keepdims=True))
        mix.append(dot_tn(low(pw[p]).reshape(256, 128), vst[p]))
    ow = low(jnp.concatenate(mix, 1))
    x = w_in + dot(ow, wcols(*BO))
    xhat2, sc2 = norm_stats(x)
    m2 = low(xhat2 * f2 + c2)
    value, slope = gelu_both(dot(m2, wcols(*BU)))
    aw = low(value)
    out_y[...] = low(x + dot_nt(aw, wcols(*BD)))

    gy = cot[...]
    dy = gy.astype(F32)
    rw = lay.rw
    unit_w = max(1, 16 // rw)
    waiting = {}

    def put_w(at, blocks):
        waiting.update({at + k: b for k, b in enumerate(blocks)})
        for first in range(0, lay.jw, unit_w):
            ready = range(first, first + unit_w)
            if all(j in waiting for j in ready):
                pack_blocks(PBw, first, [waiting.pop(j) for j in ready], rw)

    for k in range(0, FF, 512):
        put_w((BD[0] + k) // 128, columns(dot_tn(gy, aw[:, k : k + 512])))
    gzw = low(slope * dot(gy, wcols(*BD)))
    for k in range(0, FF, 512):
        put_w((BU[0] + k) // 128, columns(dot_tn(m2, gzw[:, k : k + 512])))
    dm2 = dot_nt(gzw, wcols(*BU))
    gf2 = jnp.sum(dm2 * xhat2, 0, keepdims=True)
    gc2 = jnp.sum(dm2, 0, keepdims=True)
    dx = dy + norm_back(dm2, xhat2, sc2, f2)
    gx = low(dx)
    put_w(BO[0] // 128, columns(dot_tn(ow, gx)))
    gow = low(dot_nt(gx, wcols(*BO)))
    gq, gk, gv = [], [], []
    for p in range(NP):
        go = gow[:, p * 128 : (p + 1) * 128]
        dp = dot_nt(vst[p], go).reshape(2, 128, 128)
        inner = jnp.sum(pw[p] * dp, 1, keepdims=True)
        gs = low(pw[p] * (dp - inner)).reshape(256, 128)
        gq.append(dot_tn(gs, kst[p]) * 0.125)
        gk.append(dot(side_by_side(gs, 128), qst[p]) * 0.125)
        gv.append(dot(side_by_side(low(pw[p]).reshape(256, 128), 128), head_stack(go, heads)))
    tg = low(jnp.concatenate(gq + gk + gv, 1))
    for k in range(0, 3 * D, 512):
        put_w(k // 128, columns(dot_tn(m1, tg[:, k : k + 512])))
    dm1 = dot_nt(tg, wcols(*BQ))
    gf1 = jnp.sum(dm1 * xhat1, 0, keepdims=True)
    gc1 = jnp.sum(dm1, 0, keepdims=True)
    dw = dx + norm_back(dm1, xhat1, sc1, f1)
    vec_rows = low(jnp.concatenate([gf1, gc1, gf2, gc2, jnp.zeros((12, D), F32)], 0))
    zero_w = [jnp.zeros((D, 128), F32)] * (lay.jw - lay.bw - 1)
    put_w(lay.bw, [dot_tn(vec_rows, eye)] + zero_w)
    rs_w = Scatter(g, PBw, recv[0:6], Sems(ssx, rsx), half_of(PBw.shape[4]))
    rs_w.start()

    gw = low(dw)
    grad_pr = dot_tn(pooled_low, gw)
    dpool = dot_nt(gw, Wc[:, PR])
    dp4 = jnp.concatenate([low(jnp.where(head_c[h], dpool, 0.0)) for h in range(CH)], 0)
    Ys[...] = dot_nt(dp4, Wc[:, PV]).reshape(CH, LEN, C)
    grad_pv = dot_tn(low(Us[...]).reshape(CH * LEN, C), dp4)
    for ref in (accq, acco, accu, accd, acct, sums, tsum):
        ref[...] = jnp.zeros(ref.shape, F32)

    map32 = map_hi[:32]
    GB = BWD_ROWS // 128

    def back_ffn(i, _):
        rows = pl.ds(pl.multiple_of(i * BWD_ROWS, BWD_ROWS), BWD_ROWS)
        parts = []
        for k in range(GB):
            r = i * GB + k
            own = r2s[pl.ds(pl.multiple_of(r * 128, 128), 128), :]
            alpha = alphas[pl.ds(pl.multiple_of(r * 128, 128), 128), :][:, :32]
            yg = low(
                jnp.concatenate(
                    [Ys[h, pl.ds(pl.multiple_of(r * 8, 8), 8), :] for h in range(CH)], 0
                )
            )
            da = dot_nt(own, yg)
            dr = low(alpha * (da - jnp.sum(alpha * da, 0, keepdims=True)))
            tsum[...] += dot_tn(dr, own)
            parts.append(dot(low(alpha), yg) + dot(dr, map32))
        dr2 = jnp.concatenate(parts, 0)
        g2 = low(dr2)
        accd[...] += dot_tn(g2, acts[rows, :])
        gz = low(slopes[rows, :].astype(F32) * dot(g2, Wc[:, AD]))
        accu[...] += dot_tn(n2s[rows, :], gz)
        dn = dot_nt(gz, Wc[:, AU])
        xhat = xh2[rows, :].astype(F32)
        sums[2:3, :] += jnp.sum(dn * xhat, 0, keepdims=True)
        sums[3:4, :] += jnp.sum(dn, 0, keepdims=True)
        dr1s[rows, :] = dr2 + norm_back(dn, xhat, scales[rows, 1:2], gain2)
        return 0

    nb = LEN * W // BWD_ROWS
    lax.fori_loop(0, nb // 2, back_ffn, 0)
    rs_w.step2()
    lax.fori_loop(nb // 2, nb, back_ffn, 0)
    rs_w.step3()

    t_low = low(tsum[...])
    grad_pk = dot_tn(t_low, low(pq_rows[:32]))
    rc = lay.rc
    pad1 = [jnp.zeros((C, 128), F32)] * (lay.j1 - 24)
    pack_blocks(
        PB1,
        0,
        columns(accu[...]) + columns(accd[...]) + columns(grad_pk) + columns(grad_pv)
        + columns(grad_pr) + pad1,
        rc,
    )
    rs_1 = Scatter(g, PB1, recv[6:12], Sems(ss1, rs1), half_of(PB1.shape[4]))
    rs_1.start()
    gpq = dot(t_low, Wc[:, PK]) * 0.125
    gpq = jnp.sum(
        jnp.where(iota((32, C), 0) // 8 == iota((32, C), 1) // HD, gpq, 0.0), 0, keepdims=True
    )

    def back_attention(i, _):
        rows = pl.ds(pl.multiple_of(i * BWD_ROWS, BWD_ROWS), BWD_ROWS)
        dr1 = dr1s[rows, :]
        g1 = low(dr1)
        acco[...] += dot_tn(os[rows, :], g1)
        go = low(dot_nt(g1, Wc[:, AO]))
        qkv = qkvs[rows, :]
        grads = [[], [], []]
        for k in range(GB):
            part = [[], [], []]
            for p in range(2):
                at = slice(k * 128, (k + 1) * 128)
                q, kk, v = (
                    qkv[at, b * C + p * 128 : b * C + (p + 1) * 128] for b in range(3)
                )
                gop = go[at, p * 128 : (p + 1) * 128]
                prob = probs[i * GB + k, 2 * p : 2 * p + 2]
                dp = own_word(dot_nt(head_stack(v, heads), gop), lane_word)
                gs = low(prob * (dp - jnp.sum(prob * dp, 1, keepdims=True)))
                gs = spread_words(gs, word_rows)
                pb = spread_words(low(prob), word_rows)
                part[0].append(dot_tn(gs, head_stack(kk, heads)) * 0.125)
                part[1].append(dot(side_by_side(gs, 128), head_stack(q, heads)) * 0.125)
                part[2].append(dot(side_by_side(pb, 128), head_stack(gop, heads)))
            for b in range(3):
                grads[b].append(jnp.concatenate(part[b], 1))
        tg = low(jnp.concatenate([jnp.concatenate(b, 0) for b in grads], 1))
        accq[...] += dot_tn(n1s[rows, :], tg)
        dn = dot_nt(tg, Wc[:, AQ])
        xhat = xh1[rows, :].astype(F32)
        sums[0:1, :] += jnp.sum(dn * xhat, 0, keepdims=True)
        sums[1:2, :] += jnp.sum(dn, 0, keepdims=True)
        ge = low(dr1 + norm_back(dn, xhat, scales[rows, 0:1], gain1))
        for k, h in enumerate(onehots(i, GB)):
            acct[...] += dot(h, ge[k * 128 : (k + 1) * 128])
        return 0

    lax.fori_loop(0, nb // 2, back_attention, 0)
    rs_w.step4()
    rs_1.step2()
    lax.fori_loop(nb // 2, nb, back_attention, 0)
    rs_1.step3()

    small = low(jnp.concatenate([acct[VOCAB : VOCAB + 8], sums[0:4], gpq, jnp.zeros((3, C), F32)], 0))
    pad2 = [jnp.zeros((C, 128), F32)] * (lay.j2 - 11)
    pack_blocks(
        PB2,
        0,
        columns(accq[...]) + columns(acco[...]) + columns(acct[0:VOCAB, :])
        + [dot_tn(small, eye)] + pad2,
        rc,
    )
    rs_2 = Scatter(g, PB2, recv[12:18], Sems(ss2, rs2), half_of(PB2.shape[4]))
    rs_2.start()
    rs_1.step4()
    rs_2.step2()
    rs_2.step3()

    def put(out, blocks, j, value):
        if value.shape[0] == 1:
            out[j : j + 1, :] = value
        else:
            out[pl.ds(j, value.shape[0], stride=blocks), :] = value

    def place_w(j, value):
        if j < lay.bw:
            put(out_wm, lay.bw, j, value)
        else:
            out_wvec[...] = value[:, 0:4]

    def place_1(j, value):
        put(out_cm, lay.bc, 8 + j, value)

    def place_2(j, value):
        if j < 8:
            put(out_cm, lay.bc, j, value)
        elif j < 10:
            out_lookup[:, (j - 8) * 128 : (j - 7) * 128] = value
        else:
            out_group[...] = value[:, 0:LANGS]
            out_vec[...] = value[:, LANGS : LANGS + 5]

    rs_w.finish(place_w, rw, lay.bw + 1)
    rs_1.finish(place_1, rc, 24)
    rs_2.step4()
    rs_2.finish(place_2, rc, 11)
    for part in (ag_c, ag_w, rs_w, rs_1, rs_2):
        part.drain()


def shards(
    sizes,
    char_codes,
    char_counts,
    word_groups,
    valid_words,
    char_matrix,
    char_lookup,
    group_lookup,
    char_vectors,
    word_matrix,
    word_vectors,
    cotangent,
):
    lay = Layout(sizes)
    Y, Z, X = sizes
    counts = char_counts[0]
    ints = jnp.concatenate(
        [
            char_codes.reshape(16, 128),
            jnp.repeat(word_groups.reshape(16, 8), W, 1),
            jnp.repeat(counts.reshape(16, 8), W, 1),
            jnp.tile(counts.reshape(16, 8), (1, 16)),
            jnp.broadcast_to(valid_words[:, None], (8, 128)),
        ]
    )
    exc = jnp.concatenate(
        [char_lookup, group_lookup, char_vectors, jnp.zeros((lay.rc, 128 - LANGS - 5), BF16)], 1
    ).astype(F32)
    exw = jnp.pad(word_vectors.astype(F32), ((0, 0), (0, 124)))

    def vm(shape, dtype):
        return pltpu.VMEM(shape, dtype)

    rows = LEN * W
    rows1, rows2, rowsw = lay.j1 * lay.rc, lay.j2 * lay.rc, lay.jw * lay.rw
    nag, nrs = ag_count(Y, Z, X), rs_count(Y, Z, X)
    scratch = [
        vm(lay.lead + (lay.jc * lay.rc, 128), BF16),
        vm(lay.lead + (rowsw, 128), BF16),
        vm((C, lay.jc * 128), BF16),
        vm((D, lay.jw * 128) if lay.rw < 16 else (16, 128), BF16),
        vm(lay.lead + (rows1, 128), BF16),
        vm(lay.lead + (rows2, 128), BF16),
        vm(lay.lead + (rowsw, 128), BF16),
        vm(char_matrix.shape, F32),
        vm(word_matrix.shape, F32),
        vm((rows, C), BF16),
        vm((rows, C), BF16),
        vm((rows, 3 * C), BF16),
        vm((16, CH, W, 128), F32),
        vm((rows, C), BF16),
        vm((rows, C), BF16),
        vm((rows, C), BF16),
        vm((rows, CM), BF16),
        vm((rows, CM), BF16),
        vm((rows, C), BF16),
        vm((rows, 128), F32),
        vm((rows, 128), F32),
        vm((rows, C), F32),
        vm((CH, LEN, C), F32),
        vm((CH, LEN, C), F32),
        vm((C, 3 * C), F32),
        vm((C, C), F32),
        vm((C, CM), F32),
        vm((C, CM), F32),
        vm((VOCAB + 16, C), F32),
        vm((8, C), F32),
        vm((32, C), F32),
        pltpu.SemaphoreType.DMA((1,)),
    ]
    for n in (nag, nag, nrs, nrs, nrs):
        scratch += [pltpu.SemaphoreType.DMA((n,))] * 2
    for r in (rowsw, rows1, rows2):
        scratch += rs_scratch(Y, Z, X, r, half_of(r))
    vmem = pl.BlockSpec(memory_space=pltpu.VMEM)
    outs = [
        jax.ShapeDtypeStruct((LEN, D), BF16),
        jax.ShapeDtypeStruct(char_matrix.shape, F32),
        jax.ShapeDtypeStruct(char_lookup.shape, F32),
        jax.ShapeDtypeStruct(group_lookup.shape, F32),
        jax.ShapeDtypeStruct(char_vectors.shape, F32),
        jax.ShapeDtypeStruct(word_matrix.shape, F32),
        jax.ShapeDtypeStruct(word_vectors.shape, F32),
    ]
    got = pl.pallas_call(
        functools.partial(mono, lay, STAGE),
        out_shape=outs,
        in_specs=[vmem] * 6,
        out_specs=[vmem] * 7,
        scratch_shapes=scratch,
        compiler_params=pltpu.CompilerParams(
            collective_id=0, has_side_effects=True, vmem_limit_bytes=VMEM_LIMIT
        ),
        name="layer",
    )(ints, char_matrix, exc, word_matrix, exw, cotangent[0])
    return (got[0][None],) + tuple(got[1:])


def solution(mesh):
    dp, fsdp = mesh.shape["dp"], mesh.shape["fsdp"]
    Y = dp // 2
    X = Y if fsdp % Y == 0 else 1
    sizes = (Y, fsdp // X, X)
    placed = (
        P(("dp", "fsdp"), None, None),
        P(("dp", "fsdp"), None),
        P(("dp", "fsdp"), None),
        P(("dp", "fsdp")),
        P(("dp", "fsdp"), None),
        P(("dp", "fsdp"), None),
        P(("dp", "fsdp"), None),
        P(("dp", "fsdp"), None),
        P(("dp", "fsdp"), None),
        P(("dp", "fsdp"), None),
        P(("dp", "fsdp"), None, None),
    )
    return jax.shard_map(
        functools.partial(shards, sizes),
        mesh=mesh,
        in_specs=placed,
        out_specs=(
            P(("dp", "fsdp"), None, None),
            P(("dp", "fsdp"), None),
            P(("dp", "fsdp"), None),
            P(("dp", "fsdp"), None),
            P(("dp", "fsdp"), None),
            P(("dp", "fsdp"), None),
            P(("dp", "fsdp"), None),
        ),
        check_vma=False,
    )
```

profile of v0, /device:TPU:0, one launch (start us, length us, event | category | flops | bytes accessed | tf_op | source)
XLA Modules:
  0.0 167.0 jit_solution(11281729388296909326)
XLA Ops:
  1.3 0.5 broadcast.12
  1.8 0.1 copy-done.10
  1.9 0.7 reduce.7
  2.6 0.7 reduce.6
  3.3 0.1 pad.11.clone
  3.4 0.6 copy-done.9
  4.0 0.1 copy.24
  4.1 0.6 pad_convert_fusion.exw
  4.7 0.1 reshape_squeeze.3
  4.8 0.1 copy.22
  4.8 0.1 reshape.32
  4.9 0.6 copy-done.6
  5.6 0.7 maximum_convert_fusion.exc
  6.2 0.1 broadcast_in_dim.20
  6.3 0.1 reshape.33
  6.4 0.1 broadcast_in_dim.21
  6.5 0.1 reshape.34
  6.6 0.1 copy.23
  6.6 0.6 copy-done.2
  7.3 0.1 copy.21
  7.4 0.1 reshape.31
  7.5 0.6 copy-done.1
  8.1 151.6 %layer.1 = (bf16[128,512]{1,0:T(8,128)(2,1)}, f32[256,128]{1,0:T(8,128)}, f32[8,256]{1,0:T(8,128)}, f32[8,8]{1,0:T(8,128)}, f32[8,5]{1,0:T(8,128)}, /*index=5*/f32[768,128]{1,0:T(8,128)}, f32[16,4]{1,0:T(8,128)}) custom-call(s32[72,128]{1,0:T(8,128)} %copy-done.1, bf16[256,128]{1,0:T(8,128)(2,1)} %cm.1, f32[8,384]{1,0:T(8,128)} %maximum_convert_fusion.exc, ...), custom_call_target="tpu_custom_call" | custom-call | tf_op jit(solution)/shard_map/layer/pallas_call | solution.py:872
  159.8 1.4 copy.25
  161.2 1.6 copy.37
  162.7 1.6 copy.38
  164.3 0.6 copy.39
  164.9 0.1 copy-done.5
  165.0 0.6 copy.40
  165.6 0.1 copy-done.4
  165.7 0.6 copy.41
  166.3 0.7 copy.42
  (24 shorter events, 0.1 us)
Async XLA Ops:
  1.3 0.7 copy-start.10
  1.9 0.7 copy-start.11
  3.3 0.7 copy-start.9
  4.8 0.7 copy-start.6
  4.8 0.7 copy-start.7
  4.8 0.7 copy-start.8
  6.6 0.7 copy-start.2
  7.5 0.6 copy-start.1
  159.8 6.5 %copy-start = (f32[768,128]{1,0:T(8,128)S(1)}, f32[768,128]{1,0:T(8,128)}, u32[]{:S(2)}) copy-start(f32[768,128]{1,0:T(8,128)} %get-tuple-element.47) | copy-start | bytes 1179652
  162.7 1.6 copy-start.3
  164.3 0.7 copy-start.5
  165.0 0.7 copy-start.4
where the time goes:
time: 167 us
  Pallas kernels  152 us (91%)
  local copies, waits for them, and re-layouts  11.4 us (7%)
  other arithmetic  2.62 us (2%)
    pallas_call x1, Pallas kernels, shards(): pl.pallas_call(functools.partial(mono, lay, STAGE), out_shape=outs, in_sp...  152 us
    unnamed x38, local copies, waits for them, and re-layouts  10.6 us

commit v1 on v0

v1 whole, which is shorter than its diff:
```python
import functools

import jax
import jax.numpy as jnp
from jax import lax
from jax.experimental import pallas as pl
from jax.experimental.pallas import tpu as pltpu
from jax.sharding import PartitionSpec as P

C = 256
HD = 64
CH = 4
CM = 1024
D = 512
H = 8
FF = 2048
W = 16
VOCAB = 256
LANGS = 8
LEN = 128
C_COLS = 6 * C + 2 * CM + D
D_COLS = 4 * D + 2 * FF
EPSILON = 1e-05
NEGATIVE = -1000000000.0
F32 = jnp.float32
BF16 = jnp.bfloat16
FWD_ROWS = 256
BWD_ROWS = 256
AG_PARTS_C = 2
AG_PARTS_W = 3
VMEM_LIMIT = 63 << 20
STAGE = 0


MESH = pl.DeviceIdType.MESH
ALL = slice(None)


class Grid:
    def __init__(self, sizes):
        self.Y, self.Z, self.X = sizes
        dp, fs = lax.axis_index("dp"), lax.axis_index("fsdp")
        self.y, self.c = dp // 2, dp % 2
        self.z, self.x = fs // self.X, fs % self.X
        self.me = (self.y, self.c, self.z, self.x)
        self.ys = [(self.y + k) % self.Y for k in range(1, self.Y)]
        self.zs = [(self.z + k) % self.Z for k in range(1, self.Z)]
        self.xs = [(self.x + k) % self.X for k in range(1, self.X)]
        self.to_y = [self.at(y=y) for y in self.ys]
        self.to_z = [self.at(z=z) for z in self.zs]
        self.to_x = [self.at(x=x) for x in self.xs]
        self.to_c = self.at(c=1 - self.c)

    def at(self, y=None, c=None, z=None, x=None):
        y = self.y if y is None else y
        c = self.c if c is None else c
        z = self.z if z is None else z
        x = self.x if x is None else x
        return (y * 2 + c, z * self.X + x)

    def greet(self):
        barrier = pltpu.get_barrier_semaphore()
        partners = [self.to_c] + self.to_y + self.to_z + self.to_x
        for p in partners:
            pl.semaphore_signal(barrier, inc=1, device_id=p, device_id_type=MESH)
        pl.semaphore_wait(barrier, len(partners))


class Copies:
    def __init__(self, send, recv):
        self.send, self.recv, self.made = send, recv, []

    def plan(self, src, dst, to):
        self.made.append((src, dst, to))
        return len(self.made) - 1

    def make(self, i):
        src, dst, to = self.made[i]
        return pltpu.make_async_remote_copy(
            src_ref=src,
            dst_ref=dst,
            send_sem=self.send.at[i],
            recv_sem=self.recv.at[i],
            device_id=to,
            device_id_type=MESH,
        )

    def start(self, which):
        for i in which:
            self.make(i).start()

    def arrived(self, which):
        for i in which:
            self.make(i).wait_recv()

    def left(self, which):
        for i in which:
            self.make(i).wait_send()


def ag_count(Y, Z, X):
    return (Z - 1) + 1 + 4 * ((X - 1) + (Y - 1))


class Gather:
    def __init__(self, g, G, copies, lo, hi):
        mid = lo + (hi - lo + 31) // 32 * 16
        both, a, b = slice(lo, hi), slice(lo, mid), slice(mid, hi)
        self.copies = copies
        first = len(copies.made)

        def plan(to, *idx):
            return copies.plan(G.at[idx], G.at[idx], to)

        y, c, z, x = g.me
        self.p1 = [plan(to, y, c, z, x, both) for to in g.to_z]
        self.p2a = [plan(to, y, c, ALL, x, a) for to in g.to_x]
        self.p2b = [plan(to, y, c, ALL, x, b) for to in g.to_y]
        self.c1 = [plan(g.to_c, y, c, ALL, x, both)]
        self.p3a = [plan(to, y, c, ALL, ALL, a) for to in g.to_y]
        self.p3b = [plan(to, ALL, c, ALL, x, b) for to in g.to_x]
        self.c2a = [plan(g.to_c, y, c, ALL, v, a) for v in g.xs]
        self.c2b = [plan(g.to_c, v, c, ALL, x, b) for v in g.ys]
        self.c3a = [plan(g.to_c, v, c, ALL, ALL, a) for v in g.ys]
        self.c3b = [plan(g.to_c, ALL, c, ALL, v, b) for v in g.xs]
        self.mine = range(first, len(copies.made))

    def start(self):
        self.copies.start(self.p1)

    def step2(self):
        self.copies.arrived(self.p1)
        self.copies.start(self.p2a + self.p2b + self.c1)

    def step3(self):
        self.copies.arrived(self.p2a)
        self.copies.start(self.p3a)
        self.copies.arrived(self.p2b)
        self.copies.start(self.p3b + self.c2a + self.c2b)

    def step4(self):
        self.copies.arrived(self.p3a)
        self.copies.start(self.c3a)
        self.copies.arrived(self.p3b)
        self.copies.start(self.c3b)

    def finish(self):
        self.copies.arrived(self.c1 + self.c2a + self.c2b + self.c3a + self.c3b)

    def drain(self):
        self.copies.left(self.mine)


def rs_count(Y, Z, X):
    return 1 + 2 * ((X - 1) + (Y - 1)) + 2 * (Z - 1)


def rs_scratch(Y, Z, X, rows):
    a = (rows + 31) // 32 * 16
    b = max(rows - a, 16)
    return [
        pltpu.VMEM((Y, Z, X, rows, 128), BF16),
        pltpu.VMEM((Y - 1, Z, X, a, 128), BF16),
        pltpu.VMEM((X - 1, Z, a, 128), BF16),
        pltpu.VMEM((X - 1, Y, Z, b, 128), BF16),
        pltpu.VMEM((Y - 1, Z, b, 128), BF16),
        pltpu.VMEM((Z - 1, rows, 128), BF16),
    ]


def add_into(dst, srcs):
    lead = dst.shape[:-2]
    total = 1
    for n in lead:
        total *= n

    def body(i, _):
        idx, r = [], i
        for n in reversed(lead):
            idx.append(r % n)
            r = r // n
        idx = tuple(reversed(idx))
        acc = dst[idx].astype(F32)
        for s in srcs:
            acc = acc + s[idx].astype(F32)
        dst[idx] = acc.astype(BF16)
        return 0

    lax.fori_loop(0, total, body, 0)


class Scatter:
    def __init__(self, g, PB, recv, copies, lo, hi):
        mid = lo + (hi - lo + 31) // 32 * 16
        both, a, b = slice(lo, hi), slice(lo, mid), slice(mid, hi)
        self.g, self.PB, self.copies = g, PB, copies
        self.lo, self.both, self.a, self.b = lo, both, a, b
        self.r1, self.r2a, self.r3a, self.r2b, self.r3b, self.r4 = recv
        first = len(copies.made)
        y, c, z, x = g.me

        def plan(to, dst, *idx):
            return copies.plan(PB.at[idx], dst, to)

        self.p1 = [plan(g.to_c, self.r1, ALL, 1 - c, ALL, ALL, both)]
        self.p2a = [plan(to, self.r2a.at[k], g.ys[k], c, ALL, ALL, a) for k, to in enumerate(g.to_y)]
        self.p2b = [plan(to, self.r2b.at[k], ALL, c, ALL, g.xs[k], b) for k, to in enumerate(g.to_x if mid < hi else [])]
        self.p3a = [plan(to, self.r3a.at[k], y, c, ALL, g.xs[k], a) for k, to in enumerate(g.to_x)]
        self.p3b = [plan(to, self.r3b.at[k], g.ys[k], c, ALL, x, b) for k, to in enumerate(g.to_y if mid < hi else [])]
        ra, rb = slice(0, mid - lo), slice(mid - lo, hi - lo)
        self.p4a = [plan(to, self.r4.at[k, ra], y, c, g.zs[k], x, a) for k, to in enumerate(g.to_z)]
        self.p4b = [plan(to, self.r4.at[k, rb], y, c, g.zs[k], x, b) for k, to in enumerate(g.to_z if mid < hi else [])]
        self.mine = range(first, len(copies.made))

    def start(self):
        self.copies.start(self.p1)

    def step2(self):
        c = self.g.c
        self.copies.arrived(self.p1)
        add_into(self.PB.at[:, c, :, :, self.both], [self.r1])
        self.copies.start(self.p2a + self.p2b)

    def step3(self):
        y, c, z, x = self.g.me
        self.copies.arrived(self.p2a)
        add_into(self.PB.at[y, c, :, :, self.a], [self.r2a.at[k] for k in range(len(self.p2a))])
        self.copies.start(self.p3a)
        self.copies.arrived(self.p2b)
        if self.p2b:
            add_into(self.PB.at[:, c, :, x, self.b], [self.r2b.at[k] for k in range(len(self.p2b))])
        self.copies.start(self.p3b)

    def step4(self):
        y, c, z, x = self.g.me
        self.copies.arrived(self.p3a)
        add_into(self.PB.at[y, c, :, x, self.a], [self.r3a.at[k] for k in range(len(self.p3a))])
        self.copies.start(self.p4a)
        self.copies.arrived(self.p3b)
        if self.p3b:
            add_into(self.PB.at[y, c, :, x, self.b], [self.r3b.at[k] for k in range(len(self.p3b))])
        self.copies.start(self.p4b)

    def finish(self, place, rows, count):
        self.copies.arrived(self.p4a + self.p4b)
        unit = max(1, 16 // rows)
        for t in range(-(-count // unit)):
            r = slice(t * unit * rows, (t + 1) * unit * rows)
            own = slice(self.lo + r.start, self.lo + r.stop)
            acc = self.PB[self.g.me + (own,)].astype(F32)
            for k in range(len(self.p4a)):
                acc = acc + self.r4[k, r].astype(F32)
            for u in range(unit):
                if t * unit + u < count:
                    place(t * unit + u, acc[u * rows : (u + 1) * rows])

    def drain(self):
        self.copies.left(self.mine)


def dot(a, b):
    return lax.dot_general(a, b, (((1,), (0,)), ((), ())), preferred_element_type=F32)


def dot_nt(a, b):
    return lax.dot_general(a, b, (((1,), (1,)), ((), ())), preferred_element_type=F32)


def dot_tn(a, b):
    return lax.dot_general(a, b, (((0,), (0,)), ((), ())), preferred_element_type=F32)


def low(v):
    return v.astype(BF16)


def norm_stats(x):
    centre = x - jnp.mean(x, -1, keepdims=True)
    spread = jnp.mean(centre * centre, -1, keepdims=True)
    scale = lax.rsqrt(spread + EPSILON)
    return centre * scale, scale


def norm_back(grad, xhat, scale, gain):
    inner = grad * gain
    first = jnp.mean(inner, -1, keepdims=True)
    second = jnp.mean(inner * xhat, -1, keepdims=True)
    return scale * (inner - first - xhat * second)


def gelu_both(z):
    sq = z * z
    t = jnp.tanh(z * (0.7978845608028654 + (0.7978845608028654 * 0.044715) * sq))
    h = 0.5 * z
    value = h + h * t
    slope = 0.5 + 0.5 * t + h * (1.0 - t * t) * (
        0.7978845608028654 + (3.0 * 0.7978845608028654 * 0.044715) * sq
    )
    return value, slope


def iota(shape, dim):
    return lax.broadcasted_iota(jnp.int32, shape, dim)


def head_rows(dtype):
    lane = iota((1, 128), 1)
    return [(lane // HD == h).astype(F32).astype(dtype) for h in range(2)]


def head_stack(block, heads):
    return jnp.concatenate([block * h for h in heads], 0)


def own_word(scores, lane_word):
    split = scores.reshape(2, 8, W, 128)
    out = split[:, 0]
    for w in range(1, 8):
        out = jnp.where(lane_word == w, split[:, w], out)
    return out


def spread_words(compact, word_rows):
    return jnp.concatenate([compact[h] * word_rows[w] for h in range(2) for w in range(8)], 0)


def side_by_side(stacked, rows):
    return jnp.concatenate([stacked[h * rows : (h + 1) * rows] for h in range(2)], 1)


def place_own(own, raw, staged, extra, rows, blocks, total):
    staged[...] = raw[...].astype(F32)
    unit = max(1, 16 // rows)

    def block(j):
        if j < blocks:
            if rows == 1:
                return staged[j : j + 1, :]
            return staged[pl.ds(j, rows, stride=blocks), :]
        at = (j - blocks) * 128
        if at < extra.shape[1]:
            return extra[:, at : at + 128]
        return jnp.zeros((rows, 128), F32)

    for t in range(total // unit):
        tile = jnp.concatenate([block(j) for j in range(t * unit, (t + 1) * unit)], 0)
        own[t * unit * rows : (t + 1) * unit * rows, :] = low(tile)


def assemble(G, Wd, rows, total, wide, thin):
    unit = max(1, 16 // rows)
    Y, two, Z, X = G.shape[:4]
    some = Z * X * rows

    def body(i, _):
        at = pl.ds(pl.multiple_of(i * some, 16), some)
        for t in range(total // unit):
            tile = G[i // two, i % two, :, :, t * unit * rows : (t + 1) * unit * rows, :]
            tile = tile.reshape(Z * X, 16, 128).astype(F32)
            if rows < 8:
                wide[0 : Z * X * 16, :] = tile.reshape(Z * X * 16, 128)
            for u in range(unit):
                j = t * unit + u
                if j * 128 >= Wd.shape[1]:
                    continue
                if rows < 8:
                    for r in range(rows):
                        own = wide[pl.ds(u * rows + r, Z * X, stride=16), :]
                        thin[pl.ds(r, Z * X, stride=rows) if rows > 1 else ALL, :] = own
                    Wd[at, j * 128 : (j + 1) * 128] = low(thin[...])
                    continue
                Wd[at, j * 128 : (j + 1) * 128] = low(
                    tile[:, u * rows : (u + 1) * rows, :].reshape(some, 128)
                )
        return 0

    lax.fori_loop(0, Y * two, body, 0)


def pack_blocks(PB, at, blocks, rows, wide, thick):
    unit = max(1, 16 // rows)
    lead = PB.shape[:4]
    Y, two, Z, X = lead
    devices = Y * two * Z * X
    for t in range(len(blocks) // unit):
        row = (at + t * unit) * rows
        some = blocks[t * unit : (t + 1) * unit]
        if rows >= 8:
            parts = [b.reshape(devices, rows, 128) for b in some]
            tile = low(parts[0] if unit == 1 else jnp.concatenate(parts, 1))
            PB[:, :, :, :, row : row + unit * rows, :] = tile.reshape(lead + (unit * rows, 128))
            continue
        for k, b in enumerate(some):
            thick[0 : devices * rows, :] = b
            for r in range(rows):
                own = thick[pl.ds(r, devices, stride=rows) if rows > 1 else slice(0, devices), :]
                wide[pl.ds(k * rows + r, devices, stride=16), :] = own
        for i in range(Y * two):
            own = low(wide[i * Z * X * 16 : (i + 1) * Z * X * 16, :])
            PB[i // two, i % two, :, :, row : row + 16, :] = own.reshape(Z, X, 16, 128)


def columns(value):
    return [value[:, k : k + 128] for k in range(0, value.shape[1], 128)]


class Layout:
    def __init__(self, sizes):
        self.sizes = sizes
        Y, Z, X = sizes
        self.lead = (Y, 2, Z, X)
        self.devices = Y * 2 * Z * X
        self.rc = C // self.devices
        self.rw = D // self.devices
        self.bc = C_COLS // 128
        self.bw = D_COLS // 128

        def padded(n, rows):
            unit = max(1, 16 // rows)
            return max(-(-n // unit), 2) * unit

        self.jc = padded(self.bc + 3, self.rc)
        self.jw = padded(self.bw + 1, self.rw)
        self.j1 = padded(24, self.rc)
        self.j2 = self.jc - self.j1
        f = FF // 128
        self.word_cuts = (0, f, 2 * f, self.jw)
        self.word_order = (
            [4 * D // 128 + f + k for k in range(f)]
            + [4 * D // 128 + k for k in range(f)]
            + list(range(4 * D // 128))
            + [self.bw]
        )


def put(out, blocks, j, value):
    if value.shape[0] == 1:
        out[j : j + 1, :] = value
    else:
        out[pl.ds(j, value.shape[0], stride=blocks), :] = value


class Outs:
    def __init__(self, sem):
        self.sem, self.made = sem, []

    def start(self, src, dst):
        copy = pltpu.make_async_copy(src, dst, self.sem.at[len(self.made)])
        copy.start()
        self.made.append(copy)

    def wait(self):
        for copy in self.made:
            copy.wait()


def with_events(body, events):
    def step(i, carry):
        carry = body(i, carry)
        for at, acts in events.items():

            @pl.when(i == at)
            def _(acts=acts):
                for act in acts:
                    act()

        return carry

    return step


def gather_cuts(rows, parts):
    parts = max(1, min(parts, rows // 32))
    at = [rows * k // parts // 16 * 16 for k in range(parts)] + [rows]
    return [(at[k], at[k + 1]) for k in range(parts)]


def one_hot(condition):
    return condition.astype(F32).astype(BF16)


def slot_ints(codes, counts, langs, ints):
    wide = dot_tn(codes[...].astype(F32).astype(BF16), one_hot(iota((W, 128), 1) % W == iota((W, 128), 0)))
    wide = jnp.where(iota((LEN, 128), 0) % 8 == iota((LEN, 128), 1) // W, wide, 0.0)
    ints[0:16, :] = jnp.sum(wide.reshape(16, 8, 128), 1).astype(jnp.int32)
    group_row = iota((16, LEN), 0) == iota((16, LEN), 1) // 8
    by_slot = one_hot(iota((LEN, 128), 0) % 8 == iota((LEN, 128), 1) // W)
    by_word = one_hot(iota((LEN, 128), 0) % 8 == iota((LEN, 128), 1) % 8)
    count_rows = low(jnp.where(group_row, counts[...].astype(F32), 0.0))
    lang_rows = low(jnp.where(group_row, langs[...].astype(F32), 0.0))
    ints[16:32, :] = dot(lang_rows, by_slot).astype(jnp.int32)
    ints[32:48, :] = dot(count_rows, by_slot).astype(jnp.int32)
    ints[48:64, :] = dot(count_rows, by_word).astype(jnp.int32)


def mono(
    lay, stage,
    codes_in, counts_in, langs_in, length, cm_in, lookup_in, group_in, vec_in, wm_in, wvec_in, cot_in,
    y_out, cm_out, lookup_out, group_out, vec_out, wm_out, wvec_out,
    codes, counts, langs, cm, look, grp, vec, wm, wvec, cot,
    out_y, out_lookup, out_group, out_vec, out_wvec, exc, exw, ints,
    Gc, Gw, Wc, Wwt, PBw_own, out_cm, out_wm,
    xh1, n1s, qkvs, probs, os, xh2, n2s, acts, slopes, r2s, alphas, dr1s,
    Us, Ys, accq, acco, accu, accd, acct, sums, tsum,
    wide, thin_c, thin_w, thick,
    in_sem, out_sem, ag_send, ag_recv, rs_send, rs_recv, *recv,
):
    Y, Z, X = lay.sizes
    g = Grid(lay.sizes)
    PBw = PBw_own if lay.rw >= 16 else Gw
    PBc = Gc

    ins = [
        pltpu.make_async_copy(src, dst, in_sem.at[k])
        for k, (src, dst) in enumerate(
            (
                (cm_in, cm), (lookup_in, look), (group_in, grp), (vec_in, vec), (wm_in, wm),
                (wvec_in, wvec), (codes_in, codes), (counts_in, counts), (langs_in, langs), (cot_in, cot),
            )
        )
    ]
    for copy in ins:
        copy.start()
    ag = Copies(ag_send, ag_recv)
    gather_c = [Gather(g, Gc, ag, *cut) for cut in gather_cuts(Gc.shape[4], AG_PARTS_C)]
    gather_w = [Gather(g, Gw, ag, *cut) for cut in gather_cuts(Gw.shape[4], AG_PARTS_W)]
    gathers = gather_c + gather_w
    for copy in ins[0:4]:
        copy.wait()
    exc[...] = jnp.zeros(exc.shape, F32)
    exc[:, 0 : 2 * 128] = look[...].astype(F32)
    exc[:, 256 : 256 + LANGS] = grp[...].astype(F32)
    exc[:, 256 + LANGS : 256 + LANGS + 5] = vec[...].astype(F32)
    place_own(Gc.at[g.me], cm, out_cm, exc, lay.rc, lay.bc, lay.jc)
    g.greet()
    for part in gather_c:
        part.start()
    for copy in ins[4:6]:
        copy.wait()
    exw[...] = dot_tn(wvec[...], one_hot(iota((4, 128), 0) == iota((4, 128), 1)))
    place_own(Gw.at[g.me], wm, out_wm, exw, lay.rw, lay.bw, lay.jw)
    for part in gather_w:
        part.start()
    for copy in ins[6:9]:
        copy.wait()
    slot_ints(codes, counts, langs, ints)
    ca, cb = gather_c[0], gather_c[-1]
    wa, wb, wc = gather_w[0], gather_w[len(gather_w) // 2], gather_w[-1]
    for part in gather_c:
        part.step2()
    for part in gather_c:
        part.step3()
    wa.step2()
    for part in gather_c:
        part.step4()
    if wb is not wa:
        wb.step2()
    for part in gather_c:
        part.finish()
    assemble(Gc, Wc, lay.rc, lay.jc, wide, thin_c)

    eye = (iota((16, 128), 0) == iota((16, 128), 1)).astype(F32).astype(BF16)
    rows_c = dot_nt(eye, Wc[:, (lay.bc + 2) * 128 : (lay.bc + 3) * 128])
    gain1, shift1, gain2, shift2 = (rows_c[8 + k : 9 + k] for k in range(4))
    query = rows_c[12:13]
    table_low = low(jnp.where(iota((16, C), 0) < LANGS, rows_c, 0.0))
    lookup = slice(lay.bc * 128, (lay.bc + 2) * 128)
    AQ, AO = slice(0, 3 * C), slice(3 * C, 4 * C)
    AU, AD = slice(4 * C, 4 * C + CM), slice(4 * C + CM, 4 * C + 2 * CM)
    PK, PV = slice(4 * C + 2 * CM, 5 * C + 2 * CM), slice(5 * C + 2 * CM, 6 * C + 2 * CM)
    PR = slice(6 * C + 2 * CM, 6 * C + 2 * CM + D)

    lane = iota((1, 128), 1)
    lane_word = lane // W
    word_rows = [(lane_word == w).astype(F32).astype(BF16) for w in range(8)]
    heads = head_rows(BF16)
    head_of = iota((128, C), 0) % 32 // 8 == iota((128, C), 1) // HD
    pq_rows = jnp.where(head_of, query * 0.125, 0.0)
    score_map = dot_nt(low(pq_rows), Wc[:, PK])
    map_hi = low(score_map)
    map_lo = low(score_map - map_hi.astype(F32))
    key_row = iota((1, W, 1), 1)
    pool_own = iota((128, 128), 0) // W == iota((128, 128), 1) % 8
    pool_slot = iota((128, 128), 0) % W

    def onehots(i, groups):
        parts = []
        for k in range(groups):
            r = i * groups + k
            codes = ints[pl.ds(r, 1), :]
            langs = ints[pl.ds(16 + r, 1), :]
            a = (iota((VOCAB, 128), 0) == codes).astype(F32).astype(BF16)
            b = (iota((16, 128), 0) == langs).astype(F32).astype(BF16)
            parts.append(jnp.concatenate([a, b], 0))
        return parts

    GF = FWD_ROWS // 128

    def forward(i, _):
        rows = pl.ds(pl.multiple_of(i * FWD_ROWS, FWD_ROWS), FWD_ROWS)
        table = jnp.concatenate([Wc[:, lookup], table_low], 0)
        e = jnp.concatenate([dot_tn(h, table) for h in onehots(i, GF)], 0)
        xhat, scale1 = norm_stats(e)
        n1 = low(xhat * gain1 + shift1)
        xh1[rows, :] = low(xhat)
        n1s[rows, :] = n1
        qkv = low(dot(n1, Wc[:, AQ]))
        qkvs[rows, :] = qkv
        mixed = []
        for k in range(GF):
            visible = key_row < ints[pl.ds(32 + i * GF + k, 1), :].reshape(1, 1, 128)
            pair_out = []
            for p in range(2):
                q, kk, v = (
                    qkv[k * 128 : (k + 1) * 128, b * C + p * 128 : b * C + (p + 1) * 128]
                    for b in range(3)
                )
                s = own_word(dot_nt(head_stack(kk, heads), q), lane_word) * 0.125
                s = jnp.where(visible, s, NEGATIVE)
                s = jnp.exp(s - jnp.max(s, 1, keepdims=True))
                prob = s / jnp.sum(s, 1, keepdims=True)
                probs[i * GF + k, 2 * p : 2 * p + 2] = prob
                pair_out.append(dot_tn(spread_words(low(prob), word_rows), head_stack(v, heads)))
            mixed.append(jnp.concatenate(pair_out, 1))
        o = low(jnp.concatenate(mixed, 0))
        os[rows, :] = o
        r1 = e + dot(o, Wc[:, AO])
        xhat, scale2 = norm_stats(r1)
        n2 = low(xhat * gain2 + shift2)
        xh2[rows, :] = low(xhat)
        n2s[rows, :] = n2
        alphas[rows, 64:65] = scale1
        alphas[rows, 65:66] = scale2
        value, slope = gelu_both(dot(n2, Wc[:, AU]))
        act = low(value)
        acts[rows, :] = act
        slopes[rows, :] = low(slope)
        r2 = low(r1 + dot_nt(act, Wc[:, AD]))
        r2s[rows, :] = r2
        for k in range(GF):
            r = i * GF + k
            own = r2[k * 128 : (k + 1) * 128]
            s = dot_nt(own, map_hi) + dot_nt(own, map_lo)
            seen = pool_own & (pool_slot < ints[pl.ds(48 + r, 1), :])
            s = jnp.where(seen, s, NEGATIVE)
            s = jnp.where(seen, jnp.exp(s - jnp.max(s, 0, keepdims=True)), 0.0)
            alpha = s / jnp.sum(s, 0, keepdims=True)
            alphas[pl.ds(pl.multiple_of(r * 128, 128), 128), 0:32] = alpha[:, :32]
            u = dot_tn(low(alpha)[:, :32], own)
            for h in range(CH):
                Us[h, pl.ds(pl.multiple_of(r * 8, 8), 8), :] = u[8 * h : 8 * h + 8]
        return 0

    events = {
        0: [wc.step2, wa.step3],
        2: [wb.step3],
        3: [wa.step4],
        4: [wc.step3],
        5: [wb.step4],
        7: [wc.step4],
    }
    lax.fori_loop(0, LEN * W // FWD_ROWS, with_events(forward, events), 0)

    head_c = [iota((1, C), 1) // HD == h for h in range(CH)]
    pooled = sum(jnp.where(head_c[h], dot(low(Us[h]), Wc[:, PV]), 0.0) for h in range(CH))
    pooled_low = low(pooled)
    w_in = dot(pooled_low, Wc[:, PR])

    for part in gather_w:
        part.finish()
    if lay.rw >= 16:

        def wcols(lo, hi):
            return jnp.concatenate(
                [
                    Gw[:, :, :, :, j * lay.rw : (j + 1) * lay.rw, :].reshape(D, 128)
                    for j in range(lo // 128, hi // 128)
                ],
                1,
            )

    else:
        assemble(Gw, Wwt, lay.rw, lay.jw, wide, thin_w)

        def wcols(lo, hi):
            return Wwt[:, lo:hi]

    rows_w = dot_nt(eye, wcols(D_COLS, D_COLS + 128))
    f1, c1, f2, c2 = (rows_w[k : k + 1] for k in range(4))
    BQ, BO, BU, BD = (0, 3 * D), (3 * D, 4 * D), (4 * D, 4 * D + FF), (4 * D + FF, D_COLS)
    NP = H // 2

    xhat1, sc1 = norm_stats(w_in)
    m1 = low(xhat1 * f1 + c1)
    qkv = low(dot(m1, wcols(*BQ)))
    key = iota((1, 128, 1), 1)
    seen_word = (key <= iota((1, 1, 128), 2)) & (key < length[0])
    pw, kst, qst, vst, mix = [], [], [], [], []
    for p in range(NP):
        q, kk, v = (qkv[:, b * D + p * 128 : b * D + (p + 1) * 128] for b in range(3))
        kst.append(head_stack(kk, heads))
        qst.append(head_stack(q, heads))
        vst.append(head_stack(v, heads))
        s = dot_nt(kst[p], q).reshape(2, 128, 128) * 0.125
        s = jnp.where(seen_word, s, NEGATIVE)
        s = jnp.exp(s - jnp.max(s, 1, keepdims=True))
        pw.append(s / jnp.sum(s, 1, keepdims=True))
        mix.append(dot_tn(low(pw[p]).reshape(256, 128), vst[p]))
    ow = low(jnp.concatenate(mix, 1))
    x = w_in + dot(ow, wcols(*BO))
    xhat2, sc2 = norm_stats(x)
    m2 = low(xhat2 * f2 + c2)
    value, slope = gelu_both(dot(m2, wcols(*BU)))
    aw = low(value)
    out_y[...] = low(x + dot_nt(aw, wcols(*BD)))
    outs = Outs(out_sem)
    outs.start(out_y, y_out)

    ins[9].wait()
    gy = cot[...]
    dy = gy.astype(F32)
    rw = lay.rw
    unit_w = max(1, 16 // rw)
    waiting = {}

    def put_w(at, blocks):
        waiting.update({at + k: b for k, b in enumerate(blocks)})
        for first in range(0, lay.jw, unit_w):
            ready = range(first, first + unit_w)
            if all(j in waiting for j in ready):
                pack_blocks(PBw, first, [waiting.pop(j) for j in ready], rw, wide, thick)

    cuts = [c * rw for c in lay.word_cuts]
    nrecv = len(recv) // 5
    rs = Copies(rs_send, rs_recv)
    scatters = [
        Scatter(g, PBw, recv[6 * k : 6 * k + 6], rs, cuts[k], cuts[k + 1]) for k in range(3)
    ]
    cut1 = lay.j1 * lay.rc
    scatters.append(Scatter(g, PBc, recv[18:24], rs, 0, cut1))
    scatters.append(Scatter(g, PBc, recv[24:30], rs, cut1, PBc.shape[4]))
    w1, w2, w3, c1_, c2_ = scatters
    if lay.rw < 16:
        for part in gather_w:
            part.drain()
    for k in range(0, FF, 512):
        put_w(k // 128, columns(dot_tn(gy, aw[:, k : k + 512])))
    w1.start()
    gzw = low(slope * dot(gy, wcols(*BD)))
    for k in range(0, FF, 512):
        put_w((FF + k) // 128, columns(dot_tn(m2, gzw[:, k : k + 512])))
    w2.start()
    w1.step2()
    dm2 = dot_nt(gzw, wcols(*BU))
    gf2 = jnp.sum(dm2 * xhat2, 0, keepdims=True)
    gc2 = jnp.sum(dm2, 0, keepdims=True)
    dx = dy + norm_back(dm2, xhat2, sc2, f2)
    gx = low(dx)
    put_w((2 * FF + BO[0]) // 128, columns(dot_tn(ow, gx)))
    gow = low(dot_nt(gx, wcols(*BO)))
    w2.step2()
    gq, gk, gv = [], [], []
    for p in range(NP):
        go = gow[:, p * 128 : (p + 1) * 128]
        dp = dot_nt(vst[p], go).reshape(2, 128, 128)
        inner = jnp.sum(pw[p] * dp, 1, keepdims=True)
        gs = low(pw[p] * (dp - inner)).reshape(256, 128)
        gq.append(dot_tn(gs, kst[p]) * 0.125)
        gk.append(dot(side_by_side(gs, 128), qst[p]) * 0.125)
        gv.append(dot(side_by_side(low(pw[p]).reshape(256, 128), 128), head_stack(go, heads)))
    tg = low(jnp.concatenate(gq + gk + gv, 1))
    for k in range(0, 3 * D, 512):
        put_w((2 * FF + k) // 128, columns(dot_tn(m1, tg[:, k : k + 512])))
    dm1 = dot_nt(tg, wcols(*BQ))
    gf1 = jnp.sum(dm1 * xhat1, 0, keepdims=True)
    gc1 = jnp.sum(dm1, 0, keepdims=True)
    dw = dx + norm_back(dm1, xhat1, sc1, f1)
    vec_rows = low(jnp.concatenate([gf1, gc1, gf2, gc2, jnp.zeros((12, D), F32)], 0))
    zero_w = [jnp.zeros((D, 128), F32)] * (lay.jw - lay.bw - 1)
    put_w(lay.bw, [dot_tn(vec_rows, eye)] + zero_w)
    w3.start()

    for part in gather_c:
        part.drain()
    gw = low(dw)
    dpool = dot_nt(gw, Wc[:, PR])
    dp4 = jnp.concatenate([low(jnp.where(head_c[h], dpool, 0.0)) for h in range(CH)], 0)
    Ys[...] = dot_nt(dp4, Wc[:, PV]).reshape(CH, LEN, C)
    for ref in (accq, acco, accu, accd, acct, sums, tsum):
        ref[...] = jnp.zeros(ref.shape, F32)

    map32 = map_hi[:32]
    GB = BWD_ROWS // 128

    def back_ffn(i, _):
        rows = pl.ds(pl.multiple_of(i * BWD_ROWS, BWD_ROWS), BWD_ROWS)
        parts = []
        for k in range(GB):
            r = i * GB + k
            own = r2s[pl.ds(pl.multiple_of(r * 128, 128), 128), :]
            alpha = alphas[pl.ds(pl.multiple_of(r * 128, 128), 128), 0:32]
            yg = low(
                jnp.concatenate(
                    [Ys[h, pl.ds(pl.multiple_of(r * 8, 8), 8), :] for h in range(CH)], 0
                )
            )
            da = dot_nt(own, yg)
            dr = low(alpha * (da - jnp.sum(alpha * da, 0, keepdims=True)))
            tsum[...] += dot_tn(dr, own)
            parts.append(dot(low(alpha), yg) + dot(dr, map32))
        dr2 = jnp.concatenate(parts, 0)
        g2 = low(dr2)
        accd[...] += dot_tn(g2, acts[rows, :])
        gz = low(slopes[rows, :].astype(F32) * dot(g2, Wc[:, AD]))
        accu[...] += dot_tn(n2s[rows, :], gz)
        dn = dot_nt(gz, Wc[:, AU])
        xhat = xh2[rows, :].astype(F32)
        sums[2:3, :] += jnp.sum(dn * xhat, 0, keepdims=True)
        sums[3:4, :] += jnp.sum(dn, 0, keepdims=True)
        dr1s[rows, :] = dr2 + norm_back(dn, xhat, alphas[rows, 65:66], gain2)
        return 0

    def place_w(j, value):
        j = lay.word_order[j]
        if j < lay.bw:
            put(out_wm, lay.bw, j, value)
        else:
            pick = (iota((8, 128), 0) == iota((8, 128), 1)).astype(F32)
            out_wvec[...] = lax.dot_general(
                pick, value, (((1,), (1,)), ((), ())),
                precision=lax.Precision.HIGHEST, preferred_element_type=F32,
            )[0:4]

    def place_1(j, value):
        put(out_cm, lay.bc, 8 + j, value)

    def place_2(j, value):
        if j < 8:
            put(out_cm, lay.bc, j, value)
        elif j < 10:
            out_lookup[:, (j - 8) * 128 : (j - 7) * 128] = value
        else:
            out_group[...] = value[:, 0:LANGS]
            out_vec[...] = value[:, LANGS : LANGS + 5]

    def fin_w(k):
        first = lay.word_cuts[k]
        count = min(lay.word_cuts[k + 1], lay.bw + 1) - first
        return lambda: scatters[k].finish(lambda j, v: place_w(first + j, v), rw, count)

    nb = LEN * W // BWD_ROWS
    events = {
        0: [w3.step2],
        1: [w1.step3],
        3: [w2.step3],
        4: [w1.step4],
        6: [w3.step3],
        7: [w2.step4],
    }
    lax.fori_loop(0, nb, with_events(back_ffn, events), 0)

    grad_pr = dot_tn(pooled_low, gw)
    grad_pv = dot_tn(low(Us[...]).reshape(CH * LEN, C), dp4)
    t_low = low(tsum[...])
    grad_pk = dot_tn(t_low, low(pq_rows[:32]))
    rc = lay.rc
    pad1 = [jnp.zeros((C, 128), F32)] * (lay.j1 - 24)
    pack_blocks(
        PBc,
        0,
        columns(accu[...]) + columns(accd[...]) + columns(grad_pk) + columns(grad_pv)
        + columns(grad_pr) + pad1,
        rc,
        wide,
        thick,
    )
    c1_.start()
    gpq = dot(t_low, Wc[:, PK]) * 0.125
    gpq = jnp.sum(
        jnp.where(iota((32, C), 0) // 8 == iota((32, C), 1) // HD, gpq, 0.0), 0, keepdims=True
    )

    def back_attention(i, _):
        rows = pl.ds(pl.multiple_of(i * BWD_ROWS, BWD_ROWS), BWD_ROWS)
        dr1 = dr1s[rows, :]
        g1 = low(dr1)
        acco[...] += dot_tn(os[rows, :], g1)
        go = low(dot_nt(g1, Wc[:, AO]))
        qkv = qkvs[rows, :]
        grads = [[], [], []]
        for k in range(GB):
            part = [[], [], []]
            for p in range(2):
                at = slice(k * 128, (k + 1) * 128)
                q, kk, v = (
                    qkv[at, b * C + p * 128 : b * C + (p + 1) * 128] for b in range(3)
                )
                gop = go[at, p * 128 : (p + 1) * 128]
                prob = probs[i * GB + k, 2 * p : 2 * p + 2]
                dp = own_word(dot_nt(head_stack(v, heads), gop), lane_word)
                gs = low(prob * (dp - jnp.sum(prob * dp, 1, keepdims=True)))
                gs = spread_words(gs, word_rows)
                pb = spread_words(low(prob), word_rows)
                part[0].append(dot_tn(gs, head_stack(kk, heads)) * 0.125)
                part[1].append(dot(side_by_side(gs, 128), head_stack(q, heads)) * 0.125)
                part[2].append(dot(side_by_side(pb, 128), head_stack(gop, heads)))
            for b in range(3):
                grads[b].append(jnp.concatenate(part[b], 1))
        tg = low(jnp.concatenate([jnp.concatenate(b, 0) for b in grads], 1))
        accq[...] += dot_tn(n1s[rows, :], tg)
        dn = dot_nt(tg, Wc[:, AQ])
        xhat = xh1[rows, :].astype(F32)
        sums[0:1, :] += jnp.sum(dn * xhat, 0, keepdims=True)
        sums[1:2, :] += jnp.sum(dn, 0, keepdims=True)
        ge = low(dr1 + norm_back(dn, xhat, alphas[rows, 64:65], gain1))
        for k, h in enumerate(onehots(i, GB)):
            acct[...] += dot(h, ge[k * 128 : (k + 1) * 128])
        return 0

    events = {
        1: [c1_.step2, fin_w(0)],
        2: [w3.step4],
        4: [c1_.step3, fin_w(1)],
        6: [c1_.step4],
    }
    lax.fori_loop(0, nb, with_events(back_attention, events), 0)

    small = low(jnp.concatenate([acct[VOCAB : VOCAB + 8], sums[0:4], gpq, jnp.zeros((3, C), F32)], 0))
    pad2 = [jnp.zeros((C, 128), F32)] * (lay.j2 - 11)
    pack_blocks(
        PBc,
        lay.j1,
        columns(accq[...]) + columns(acco[...]) + columns(acct[0:VOCAB, :])
        + [dot_tn(small, eye)] + pad2,
        rc,
        wide,
        thick,
    )
    c2_.start()
    fin_w(2)()
    outs.start(out_wm, wm_out)
    outs.start(out_wvec, wvec_out)
    c2_.step2()
    c1_.finish(place_1, rc, 24)
    c2_.step3()
    c2_.step4()
    c2_.finish(place_2, rc, 11)
    outs.start(out_cm, cm_out)
    outs.start(out_lookup, lookup_out)
    outs.start(out_group, group_out)
    outs.start(out_vec, vec_out)
    for part in (gather_w if lay.rw >= 16 else []) + scatters:
        part.drain()
    outs.wait()


def hand_over(*refs):
    n = 7
    ins, outs, held, sems = refs[:n], refs[n : 2 * n], refs[2 * n : 3 * n], refs[-1]
    first = [pltpu.make_async_copy(ins[k], held[k], sems.at[k]) for k in range(n)]
    then = [pltpu.make_async_copy(held[k], outs[k], sems.at[n + k]) for k in range(n)]
    for copy in first:
        copy.start()
    for k in range(n):
        first[k].wait()
        then[k].start()
    for copy in then:
        copy.wait()


def shards(
    sizes,
    char_codes,
    char_counts,
    word_groups,
    valid_words,
    char_matrix,
    char_lookup,
    group_lookup,
    char_vectors,
    word_matrix,
    word_vectors,
    cotangent,
):
    lay = Layout(sizes)
    Y, Z, X = sizes
    rows = LEN * W
    rows_c, rows_w = lay.jc * lay.rc, lay.jw * lay.rw
    rows_1, rows_2 = lay.j1 * lay.rc, lay.j2 * lay.rc
    word_parts = [(b - a) * lay.rw for a, b in zip(lay.word_cuts, lay.word_cuts[1:])]
    nag = ag_count(Y, Z, X) * (AG_PARTS_C + AG_PARTS_W)
    nrs = rs_count(Y, Z, X) * 5
    dma = pltpu.SemaphoreType.DMA

    def vm(shape, dtype):
        return pltpu.VMEM(shape, dtype)

    def like(a):
        return pltpu.VMEM(a.shape, a.dtype)

    ins = (
        char_codes[0].T,
        char_counts,
        word_groups,
        valid_words,
        char_matrix,
        char_lookup,
        group_lookup,
        char_vectors,
        word_matrix,
        word_vectors.T,
        cotangent[0],
    )
    outs = [
        jax.ShapeDtypeStruct((LEN, D), BF16),
        jax.ShapeDtypeStruct(char_matrix.shape, F32),
        jax.ShapeDtypeStruct(char_lookup.shape, F32),
        jax.ShapeDtypeStruct(group_lookup.shape, F32),
        jax.ShapeDtypeStruct(char_vectors.shape, F32),
        jax.ShapeDtypeStruct(word_matrix.shape, F32),
        jax.ShapeDtypeStruct(word_vectors.shape[::-1], F32),
    ]
    scratch = [like(a) for k, a in enumerate(ins) if k != 3]
    scratch += [like(outs[k]) for k in (0, 2, 3, 4, 6)]
    scratch += [
        vm((lay.rc, 3 * 128), F32),
        vm((lay.rw, 128), F32),
        vm((64, 128), jnp.int32),
        vm(lay.lead + (rows_c, 128), BF16),
        vm(lay.lead + (rows_w, 128), BF16),
        vm((C, (lay.bc + 3) * 128), BF16),
        vm((D, (lay.bw + 1) * 128) if lay.rw < 16 else (16, 128), BF16),
        vm(lay.lead + (rows_w, 128) if lay.rw >= 16 else (16, 128), BF16),
        like(outs[1]),
        like(outs[5]),
        vm((rows, C), BF16),
        vm((rows, C), BF16),
        vm((rows, 3 * C), BF16),
        vm((16, CH, W, 128), F32),
        vm((rows, C), BF16),
        vm((rows, C), BF16),
        vm((rows, C), BF16),
        vm((rows, CM), BF16),
        vm((rows, CM), BF16),
        vm((rows, C), BF16),
        vm((rows, 128), F32),
        vm((rows, C), F32),
        vm((CH, LEN, C), F32),
        vm((CH, LEN, C), F32),
        vm((C, 3 * C), F32),
        vm((C, C), F32),
        vm((C, CM), F32),
        vm((C, CM), F32),
        vm((VOCAB + 16, C), F32),
        vm((8, C), F32),
        vm((32, C), F32),
        vm((lay.devices * 16 if lay.rc < 8 else 8, 128), F32),
        vm((Z * X * lay.rc, 128), F32),
        vm((Z * X * lay.rw, 128), F32),
        vm((D if lay.rc < 8 else 8, 128), F32),
        dma((10,)),
        dma((7,)),
        dma((nag,)),
        dma((nag,)),
        dma((nrs,)),
        dma((nrs,)),
    ]
    for n in word_parts + [rows_1, rows_2]:
        scratch += rs_scratch(Y, Z, X, n)
    anywhere = pl.BlockSpec(memory_space=pl.ANY)
    in_specs = [anywhere] * 11
    in_specs[3] = pl.BlockSpec(memory_space=pltpu.SMEM)
    got = pl.pallas_call(
        functools.partial(mono, lay, STAGE),
        out_shape=outs,
        in_specs=in_specs,
        out_specs=[anywhere] * 7,
        scratch_shapes=scratch,
        compiler_params=pltpu.CompilerParams(
            collective_id=0, has_side_effects=True, vmem_limit_bytes=VMEM_LIMIT
        ),
        name="layer",
    )(*ins)
    got = pl.pallas_call(
        hand_over,
        out_shape=outs,
        in_specs=[anywhere] * 7,
        out_specs=[anywhere] * 7,
        scratch_shapes=[like(a) for a in outs] + [dma((14,))],
        name="hand_over",
    )(*got)
    return (got[0][None],) + tuple(got[1:6]) + (got[6].T,)


def solution(mesh):
    dp, fsdp = mesh.shape["dp"], mesh.shape["fsdp"]
    Y = dp // 2
    X = Y if fsdp % Y == 0 else 1
    sizes = (Y, fsdp // X, X)
    placed = (
        P(("dp", "fsdp"), None, None),
        P(("dp", "fsdp"), None),
        P(("dp", "fsdp"), None),
        P(("dp", "fsdp")),
        P(("dp", "fsdp"), None),
        P(("dp", "fsdp"), None),
        P(("dp", "fsdp"), None),
        P(("dp", "fsdp"), None),
        P(("dp", "fsdp"), None),
        P(("dp", "fsdp"), None),
        P(("dp", "fsdp"), None, None),
    )
    return jax.shard_map(
        functools.partial(shards, sizes),
        mesh=mesh,
        in_specs=placed,
        out_specs=(
            P(("dp", "fsdp"), None, None),
            P(("dp", "fsdp"), None),
            P(("dp", "fsdp"), None),
            P(("dp", "fsdp"), None),
            P(("dp", "fsdp"), None),
            P(("dp", "fsdp"), None),
            P(("dp", "fsdp"), None),
        ),
        check_vma=False,
    )
```

time: 167 us -> 128 us (0.77)
  Pallas kernels: 152 us -> 127 us
  local copies, waits for them, and re-layouts: 11.4 us -> 0 us
  other arithmetic: 2.62 us -> 0 us
    pallas_call x1, Pallas kernels: 152 us -> 125 us  [shards(): pl.pallas_call(functools.partial(mono, lay, STAGE), out_shape=outs, in_sp...]
    unnamed x38 -> x0, local copies, waits for them, and re-layouts: 10.6 us -> none
    pallas_call x0 -> x1, Pallas kernels: none -> 2.03 us  [shards(): pl.pallas_call(hand_over, out_shape=outs, in_specs=[anywhere] * 7, out_sp...]
where the time goes in v1:
time: 128 us
  Pallas kernels  127 us (99%)
  between operations  1.45 us (1%)
    pallas_call x1, Pallas kernels, shards(): pl.pallas_call(functools.partial(mono, lay, STAGE), out_shape=outs, in_sp...  125 us

profile of v1, /device:TPU:0, one launch (start us, length us, event | category | flops | bytes accessed | tf_op | source)
XLA Modules:
  0.0 128.0 jit_solution(3947005753575771795)
XLA Ops:
  1.3 124.6 %layer.1 = (bf16[128,512]{1,0:T(8,128)(2,1)}, f32[256,128]{1,0:T(8,128)}, f32[8,256]{1,0:T(8,128)}, f32[8,8]{1,0:T(8,128)}, f32[8,5]{1,0:T(8,128)}, /*index=5*/f32[768,128]{1,0:T(8,128)}, f32[4,16]{1,0:T(4,128)}) custom-call(s32[16,128]{1,0:T(8,128)} %bitcast.8, s32[1,128]{1,0:T(1,128)} %counts_in.1, s32[1,128]{1,0:T(1,128)} %langs_in.1, s32[1]{0:T(128)S(6)} %copy.18.length, ...), custom_call_target="tpu_custom_call" | custom-call | tf_op jit(solution)/shard_map/layer/pallas_call | solution.py:1073
  125.9 2.0 %hand_over.1 = (bf16[128,512]{1,0:T(8,128)(2,1)}, f32[256,128]{1,0:T(8,128)}, f32[8,256]{1,0:T(8,128)}, f32[8,8]{1,0:T(8,128)}, f32[8,5]{1,0:T(8,128)}, /*index=5*/f32[768,128]{1,0:T(8,128)}, f32[4,16]{1,0:T(4,128)}) custom-call(bf16[128,512]{1,0:T(8,128)(2,1)} %get-tuple-element.21.refs_0_, f32[256,128]{1,0:T(8,128)} %get-tuple-element.22.refs_1_, ...), custom_call_target="tpu_custom_call" | custom-call | tf_op jit(solution)/shard_map/hand_over/pallas_call | solution.py:1084

commit v2 on v1

--- a/solution.py
+++ b/solution.py
@@ -24,10 +24,9 @@
 NEGATIVE = -1000000000.0
 F32 = jnp.float32
 BF16 = jnp.bfloat16
-FWD_ROWS = 256
-BWD_ROWS = 256
-AG_PARTS_C = 2
-AG_PARTS_W = 3
+FWD_ROWS = 512
+BWD_ROWS = 512
+FFN_ROWS = 512
 VMEM_LIMIT = 63 << 20
 STAGE = 0
 
@@ -50,6 +49,13 @@
         self.to_z = [self.at(z=z) for z in self.zs]
         self.to_x = [self.at(x=x) for x in self.xs]
         self.to_c = self.at(c=1 - self.c)
+        self.to = {"y": self.to_y, "z": self.to_z, "x": self.to_x}
+        self.src = {
+            "y": [(self.y + self.Y - k) % self.Y for k in range(1, self.Y)],
+            "z": [(self.z + self.Z - k) % self.Z for k in range(1, self.Z)],
+            "x": [(self.x + self.X - k) % self.X for k in range(1, self.X)],
+        }
+        self.off = {"y": self.ys, "z": self.zs, "x": self.xs}
 
     def at(self, y=None, c=None, z=None, x=None):
         y = self.y if y is None else y
@@ -60,10 +66,12 @@
 
     def greet(self):
         barrier = pltpu.get_barrier_semaphore()
-        partners = [self.to_c] + self.to_y + self.to_z + self.to_x
-        for p in partners:
+        self.partners = [self.to_c] + self.to_y + self.to_z + self.to_x
+        for p in self.partners:
             pl.semaphore_signal(barrier, inc=1, device_id=p, device_id_type=MESH)
-        pl.semaphore_wait(barrier, len(partners))
+
+    def met(self):
+        pl.semaphore_wait(pltpu.get_barrier_semaphore(), len(self.partners))
 
 
 class Copies:
@@ -99,73 +107,79 @@
 
 
 def ag_count(Y, Z, X):
-    return (Z - 1) + 1 + 4 * ((X - 1) + (Y - 1))
+    n = max(Z - 1, X - 1, Y - 1)
+    return 6 * n + 1 + 2 * n * n
 
 
 class Gather:
-    def __init__(self, g, G, copies, lo, hi):
-        mid = lo + (hi - lo + 31) // 32 * 16
-        both, a, b = slice(lo, hi), slice(lo, mid), slice(mid, hi)
+    def __init__(self, g, G, copies, lo, hi, order):
         self.copies = copies
         first = len(copies.made)
-
-        def plan(to, *idx):
-            return copies.plan(G.at[idx], G.at[idx], to)
-
-        y, c, z, x = g.me
-        self.p1 = [plan(to, y, c, z, x, both) for to in g.to_z]
-        self.p2a = [plan(to, y, c, ALL, x, a) for to in g.to_x]
-        self.p2b = [plan(to, y, c, ALL, x, b) for to in g.to_y]
-        self.c1 = [plan(g.to_c, y, c, ALL, x, both)]
-        self.p3a = [plan(to, y, c, ALL, ALL, a) for to in g.to_y]
-        self.p3b = [plan(to, ALL, c, ALL, x, b) for to in g.to_x]
-        self.c2a = [plan(g.to_c, y, c, ALL, v, a) for v in g.xs]
-        self.c2b = [plan(g.to_c, v, c, ALL, x, b) for v in g.ys]
-        self.c3a = [plan(g.to_c, v, c, ALL, ALL, a) for v in g.ys]
-        self.c3b = [plan(g.to_c, ALL, c, ALL, v, b) for v in g.xs]
+        one, two, three = order
+        rows = slice(lo, hi)
+
+        def slot(**at):
+            v = {"y": g.y, "z": g.z, "x": g.x, **at}
+            return (v["y"], g.c, v["z"], v["x"], rows)
+
+        def plan(to, **at):
+            return copies.plan(G.at[slot(**at)], G.at[slot(**at)], to)
+
+        self.first = [plan(to) for to in g.to[one]]
+        self.own2 = [plan(to) for to in g.to[two]]
+        self.own3 = [plan(to, **{two: ALL}) for to in g.to[three]]
+        self.rest2 = [[plan(to, **{one: v}) for to in g.to[two]] for v in g.src[one]]
+        self.rest3 = [[plan(to, **{one: v, two: ALL}) for to in g.to[three]] for v in g.src[one]]
+        self.core1 = [plan(g.to_c)]
+        self.core2 = [plan(g.to_c, **{two: w}) for w in g.src[two]]
+        self.core4 = [[plan(g.to_c, **{one: v, two: ALL})] for v in g.src[one]]
+        self.core5 = [plan(g.to_c, **{one: ALL, two: ALL, three: u}) for u in g.src[three]]
         self.mine = range(first, len(copies.made))
 
-    def start(self):
-        self.copies.start(self.p1)
+    def step1(self):
+        self.copies.start(self.first + self.own2 + self.core1)
 
     def step2(self):
-        self.copies.arrived(self.p1)
-        self.copies.start(self.p2a + self.p2b + self.c1)
+        self.copies.arrived(self.own2)
+        self.copies.start(self.own3 + self.core2)
 
     def step3(self):
-        self.copies.arrived(self.p2a)
-        self.copies.start(self.p3a)
-        self.copies.arrived(self.p2b)
-        self.copies.start(self.p3b + self.c2a + self.c2b)
+        for k, which in enumerate(self.rest2):
+            self.copies.arrived(self.first[k : k + 1])
+            self.copies.start(which)
 
     def step4(self):
-        self.copies.arrived(self.p3a)
-        self.copies.start(self.c3a)
-        self.copies.arrived(self.p3b)
-        self.copies.start(self.c3b)
+        for k, which in enumerate(self.rest3):
+            self.copies.arrived(self.rest2[k])
+            self.copies.start(which + self.core4[k])
+
+    def step5(self):
+        self.copies.arrived(self.own3)
+        for which in self.rest3:
+            self.copies.arrived(which)
+        self.copies.start(self.core5)
 
     def finish(self):
-        self.copies.arrived(self.c1 + self.c2a + self.c2b + self.c3a + self.c3b)
+        self.copies.arrived(self.core1 + self.core2 + self.core5)
+        for which in self.core4:
+            self.copies.arrived(which)
 
     def drain(self):
         self.copies.left(self.mine)
 
 
 def rs_count(Y, Z, X):
-    return 1 + 2 * ((X - 1) + (Y - 1)) + 2 * (Z - 1)
-
-
-def rs_scratch(Y, Z, X, rows):
-    a = (rows + 31) // 32 * 16
-    b = max(rows - a, 16)
-    return [
-        pltpu.VMEM((Y, Z, X, rows, 128), BF16),
-        pltpu.VMEM((Y - 1, Z, X, a, 128), BF16),
-        pltpu.VMEM((X - 1, Z, a, 128), BF16),
-        pltpu.VMEM((X - 1, Y, Z, b, 128), BF16),
-        pltpu.VMEM((Y - 1, Z, b, 128), BF16),
-        pltpu.VMEM((Z - 1, rows, 128), BF16),
-    ]
+    return 1 + (Z - 1) + (X - 1) + (Y - 1)
+
+
+def rs_scratch(sizes, rows, order):
+    n = dict(zip("yzx", sizes))
+    left = dict(n)
+    shapes = [pltpu.VMEM(sizes + (rows, 128), BF16)]
+    for axis in order:
+        left[axis] = 1
+        shapes.append(pltpu.VMEM((n[axis] - 1, left["y"], left["z"], left["x"], rows, 128), BF16))
+    return shapes
 
 
 def add_into(dst, srcs):
@@ -190,72 +204,126 @@
 
 
 class Scatter:
-    def __init__(self, g, PB, recv, copies, lo, hi):
-        mid = lo + (hi - lo + 31) // 32 * 16
-        both, a, b = slice(lo, hi), slice(lo, mid), slice(mid, hi)
-        self.g, self.PB, self.copies = g, PB, copies
-        self.lo, self.both, self.a, self.b = lo, both, a, b
-        self.r1, self.r2a, self.r3a, self.r2b, self.r3b, self.r4 = recv
+    def __init__(self, g, PB, recv, copies, lo, hi, order):
+        self.g, self.PB, self.copies, self.recv = g, PB, copies, recv
+        self.lo, self.hi = lo, hi
         first = len(copies.made)
-        y, c, z, x = g.me
-
-        def plan(to, dst, *idx):
-            return copies.plan(PB.at[idx], dst, to)
-
-        self.p1 = [plan(g.to_c, self.r1, ALL, 1 - c, ALL, ALL, both)]
-        self.p2a = [plan(to, self.r2a.at[k], g.ys[k], c, ALL, ALL, a) for k, to in enumerate(g.to_y)]
-        self.p2b = [plan(to, self.r2b.at[k], ALL, c, ALL, g.xs[k], b) for k, to in enumerate(g.to_x if mid < hi else [])]
-        self.p3a = [plan(to, self.r3a.at[k], y, c, ALL, g.xs[k], a) for k, to in enumerate(g.to_x)]
-        self.p3b = [plan(to, self.r3b.at[k], g.ys[k], c, ALL, x, b) for k, to in enumerate(g.to_y if mid < hi else [])]
-        ra, rb = slice(0, mid - lo), slice(mid - lo, hi - lo)
-        self.p4a = [plan(to, self.r4.at[k, ra], y, c, g.zs[k], x, a) for k, to in enumerate(g.to_z)]
-        self.p4b = [plan(to, self.r4.at[k, rb], y, c, g.zs[k], x, b) for k, to in enumerate(g.to_z if mid < hi else [])]
+        rows = slice(lo, hi)
+        me = {"y": g.y, "z": g.z, "x": g.x}
+        have = {"y": ALL, "z": ALL, "x": ALL}
+
+        def slot(c, **at):
+            v = {**have, **at}
+            return (v["y"], c, v["z"], v["x"], rows)
+
+        self.hops = [[copies.plan(PB.at[slot(1 - g.c)], recv[0], g.to_c)]]
+        self.sums = [PB.at[slot(g.c)]]
+        for n, axis in enumerate(order):
+            self.hops.append(
+                [
+                    copies.plan(PB.at[slot(g.c, **{axis: pl.ds(v, 1)})], recv[n + 1].at[k], to)
+                    for k, (v, to) in enumerate(zip(g.off[axis], g.to[axis]))
+                ]
+            )
+            have[axis] = pl.ds(me[axis], 1)
+            self.sums.append(PB.at[slot(g.c)])
         self.mine = range(first, len(copies.made))
 
-    def start(self):
-        self.copies.start(self.p1)
+    def add(self, n):
+        self.copies.arrived(self.hops[n])
+        if n == 0:
+            add_into(self.sums[0], [self.recv[0]])
+        else:
+            add_into(self.sums[n], [self.recv[n].at[k] for k in range(len(self.hops[n]))])
+
+    def step1(self):
+        self.copies.start(self.hops[0])
 
     def step2(self):
-        c = self.g.c
-        self.copies.arrived(self.p1)
-        add_into(self.PB.at[:, c, :, :, self.both], [self.r1])
-        self.copies.start(self.p2a + self.p2b)
+        self.add(0)
+        self.copies.start(self.hops[1])
 
     def step3(self):
-        y, c, z, x = self.g.me
-        self.copies.arrived(self.p2a)
-        add_into(self.PB.at[y, c, :, :, self.a], [self.r2a.at[k] for k in range(len(self.p2a))])
-        self.copies.start(self.p3a)
-        self.copies.arrived(self.p2b)
-        if self.p2b:
-            add_into(self.PB.at[:, c, :, x, self.b], [self.r2b.at[k] for k in range(len(self.p2b))])
-        self.copies.start(self.p3b)
+        self.add(1)
+        self.copies.start(self.hops[2])
 
     def step4(self):
-        y, c, z, x = self.g.me
-        self.copies.arrived(self.p3a)
-        add_into(self.PB.at[y, c, :, x, self.a], [self.r3a.at[k] for k in range(len(self.p3a))])
-        self.copies.start(self.p4a)
-        self.copies.arrived(self.p3b)
-        if self.p3b:
-            add_into(self.PB.at[y, c, :, x, self.b], [self.r3b.at[k] for k in range(len(self.p3b))])
-        self.copies.start(self.p4b)
-
-    def finish(self, place, rows, count):
-        self.copies.arrived(self.p4a + self.p4b)
-        unit = max(1, 16 // rows)
-        for t in range(-(-count // unit)):
-            r = slice(t * unit * rows, (t + 1) * unit * rows)
-            own = slice(self.lo + r.start, self.lo + r.stop)
-            acc = self.PB[self.g.me + (own,)].astype(F32)
-            for k in range(len(self.p4a)):
-                acc = acc + self.r4[k, r].astype(F32)
-            for u in range(unit):
-                if t * unit + u < count:
-                    place(t * unit + u, acc[u * rows : (u + 1) * rows])
+        self.add(2)
+        self.copies.start(self.hops[3])
+
+    def finish(self, place, rows, base, count):
+        self.copies.arrived(self.hops[3])
+        size = max(rows, 16)
+        for row in range(self.lo, self.hi, size):
+            r = slice(row - self.lo, row - self.lo + size)
+            acc = self.PB[self.g.me + (slice(row, row + size),)].astype(F32)
+            for k in range(len(self.hops[3])):
+                acc = acc + self.recv[3][k, 0, 0, 0, r].astype(F32)
+            for u in range(size // rows):
+                j = (row - base) // rows + u
+                if j < count:
+                    place(j, acc[u * rows : (u + 1) * rows])
 
     def drain(self):
         self.copies.left(self.mine)
+
+
+class Pair:
+    def __init__(self, parts):
+        self.parts = parts
+
+    def all(self, name, *args):
+        for part in self.parts:
+            getattr(part, name)(*args)
+
+    def step1(self):
+        self.all("step1")
+
+    def step2(self):
+        self.all("step2")
+
+    def step3(self):
+        self.all("step3")
+
+    def step4(self):
+        self.all("step4")
+
+    def step5(self):
+        self.all("step5")
+
+    def finish(self, *args):
+        self.all("finish", *args)
+
+    def drain(self):
+        self.all("drain")
+
+
+def halves(lo, hi):
+    mid = lo + (hi - lo + 31) // 32 * 16
+    return [(lo, mid), (mid, hi)] if mid < hi else [(lo, hi)]
+
+
+def gather_pair(g, G, copies, lo, hi):
+    orders = ("zxy", "zyx")
+    return Pair([Gather(g, G, copies, *cut, o) for cut, o in zip(halves(lo, hi), orders)])
+
+
+SUM_ORDERS = ("yxz", "xyz")
+
+
+def scatter_pair(g, PB, recv, copies, lo, hi):
+    parts = []
+    for cut, o in zip(halves(lo, hi), SUM_ORDERS):
+        parts.append(Scatter(g, PB, recv[:4], copies, *cut, o))
+        del recv[:4]
+    return Pair(parts)
+
+
+def scatter_pair_scratch(sizes, lo, hi):
+    out = []
+    for (a, b), o in zip(halves(lo, hi), SUM_ORDERS):
+        out += rs_scratch(sizes, b - a, o)
+    return out
 
 
 def dot(a, b):
@@ -328,40 +396,40 @@
     return jnp.concatenate([stacked[h * rows : (h + 1) * rows] for h in range(2)], 1)
 
 
-def place_own(own, raw, staged, extra, rows, blocks, total):
+def place_own(own, raw, staged, extra, rows, blocks, order):
     staged[...] = raw[...].astype(F32)
     unit = max(1, 16 // rows)
 
     def block(j):
+        if j is None:
+            return jnp.zeros((rows, 128), F32)
         if j < blocks:
             if rows == 1:
                 return staged[j : j + 1, :]
             return staged[pl.ds(j, rows, stride=blocks), :]
         at = (j - blocks) * 128
-        if at < extra.shape[1]:
-            return extra[:, at : at + 128]
-        return jnp.zeros((rows, 128), F32)
-
-    for t in range(total // unit):
-        tile = jnp.concatenate([block(j) for j in range(t * unit, (t + 1) * unit)], 0)
+        return extra[:, at : at + 128]
+
+    for t in range(len(order) // unit):
+        tile = jnp.concatenate([block(j) for j in order[t * unit : (t + 1) * unit]], 0)
         own[t * unit * rows : (t + 1) * unit * rows, :] = low(tile)
 
 
-def assemble(G, Wd, rows, total, wide, thin):
+def assemble(G, Wd, rows, order, wide, thin):
     unit = max(1, 16 // rows)
     Y, two, Z, X = G.shape[:4]
     some = Z * X * rows
 
     def body(i, _):
         at = pl.ds(pl.multiple_of(i * some, 16), some)
-        for t in range(total // unit):
+        for t in range(len(order) // unit):
             tile = G[i // two, i % two, :, :, t * unit * rows : (t + 1) * unit * rows, :]
             tile = tile.reshape(Z * X, 16, 128).astype(F32)
             if rows < 8:
                 wide[0 : Z * X * 16, :] = tile.reshape(Z * X * 16, 128)
             for u in range(unit):
-                j = t * unit + u
-                if j * 128 >= Wd.shape[1]:
+                j = order[t * unit + u]
+                if j is None:
                     continue
                 if rows < 8:
                     for r in range(rows):
@@ -420,17 +488,20 @@
             return max(-(-n // unit), 2) * unit
 
         self.jc = padded(self.bc + 3, self.rc)
-        self.jw = padded(self.bw + 1, self.rw)
         self.j1 = padded(24, self.rc)
         self.j2 = self.jc - self.j1
+        thin = self.rc < 8
+        self.fwd_rows = 256 if thin else FWD_ROWS
+        self.ffn_rows = 256 if thin else FFN_ROWS
+        self.bwd_rows = 256 if thin else BWD_ROWS
         f = FF // 128
-        self.word_cuts = (0, f, 2 * f, self.jw)
-        self.word_order = (
-            [4 * D // 128 + f + k for k in range(f)]
-            + [4 * D // 128 + k for k in range(f)]
-            + list(range(4 * D // 128))
-            + [self.bw]
-        )
+        rest = 4 * D // 128
+        up = padded(rest + 1, self.rw)
+        self.jw = up + 2 * f
+        self.word_cuts = (0, up, up + f, self.jw)
+        self.word_order = list(range(rest)) + [self.bw] + [None] * (up - rest - 1)
+        self.word_order += list(range(rest, rest + 2 * f))
+        self.word_at = {j: p for p, j in enumerate(self.word_order) if j is not None}
 
 
 def put(out, blocks, j, value):
@@ -454,25 +525,17 @@
             copy.wait()
 
 
-def with_events(body, events):
-    def step(i, carry):
-        carry = body(i, carry)
-        for at, acts in events.items():
-
-            @pl.when(i == at)
-            def _(acts=acts):
-                for act in acts:
-                    act()
-
-        return carry
-
-    return step
-
-
-def gather_cuts(rows, parts):
-    parts = max(1, min(parts, rows // 32))
-    at = [rows * k // parts // 16 * 16 for k in range(parts)] + [rows]
-    return [(at[k], at[k + 1]) for k in range(parts)]
+def hooks(events):
+    def hook(i, place):
+        for (at, where), acts in events.items():
+            if where == place:
+
+                @pl.when(i == at)
+                def _(acts=acts):
+                    for act in acts:
+                        act()
+
+    return hook
 
 
 def one_hot(condition):
@@ -499,7 +562,7 @@
     y_out, cm_out, lookup_out, group_out, vec_out, wm_out, wvec_out,
     codes, counts, langs, cm, look, grp, vec, wm, wvec, cot,
     out_y, out_lookup, out_group, out_vec, out_wvec, exc, exw, ints,
-    Gc, Gw, Wc, Wwt, PBw_own, out_cm, out_wm,
+    Gc, Gw, PBd, Wc, Wwt, out_cm, out_wm,
     xh1, n1s, qkvs, probs, os, xh2, n2s, acts, slopes, r2s, alphas, dr1s,
     Us, Ys, accq, acco, accu, accd, acct, sums, tsum,
     wide, thin_c, thin_w, thick,
@@ -507,7 +570,6 @@
 ):
     Y, Z, X = lay.sizes
     g = Grid(lay.sizes)
-    PBw = PBw_own if lay.rw >= 16 else Gw
     PBc = Gc
 
     ins = [
@@ -522,42 +584,38 @@
     for copy in ins:
         copy.start()
     ag = Copies(ag_send, ag_recv)
-    gather_c = [Gather(g, Gc, ag, *cut) for cut in gather_cuts(Gc.shape[4], AG_PARTS_C)]
-    gather_w = [Gather(g, Gw, ag, *cut) for cut in gather_cuts(Gw.shape[4], AG_PARTS_W)]
-    gathers = gather_c + gather_w
+    cuts = [c * lay.rw for c in lay.word_cuts]
+    gc = gather_pair(g, Gc, ag, 0, Gc.shape[4])
+    gu = gather_pair(g, Gw, ag, 0, cuts[2])
+    gd = gather_pair(g, Gw, ag, cuts[2], cuts[3])
+    g.greet()
     for copy in ins[0:4]:
         copy.wait()
     exc[...] = jnp.zeros(exc.shape, F32)
     exc[:, 0 : 2 * 128] = look[...].astype(F32)
     exc[:, 256 : 256 + LANGS] = grp[...].astype(F32)
     exc[:, 256 + LANGS : 256 + LANGS + 5] = vec[...].astype(F32)
-    place_own(Gc.at[g.me], cm, out_cm, exc, lay.rc, lay.bc, lay.jc)
-    g.greet()
-    for part in gather_c:
-        part.start()
+    order_c = list(range(lay.bc + 3)) + [None] * (lay.jc - lay.bc - 3)
+    place_own(Gc.at[g.me], cm, out_cm, exc, lay.rc, lay.bc, order_c)
+    g.met()
+    gc.step1()
     for copy in ins[4:6]:
         copy.wait()
     exw[...] = dot_tn(wvec[...], one_hot(iota((4, 128), 0) == iota((4, 128), 1)))
-    place_own(Gw.at[g.me], wm, out_wm, exw, lay.rw, lay.bw, lay.jw)
-    for part in gather_w:
-        part.start()
+    place_own(Gw.at[g.me], wm, out_wm, exw, lay.rw, lay.bw, lay.word_order)
+    gu.step1()
+    gd.step1()
     for copy in ins[6:9]:
         copy.wait()
     slot_ints(codes, counts, langs, ints)
-    ca, cb = gather_c[0], gather_c[-1]
-    wa, wb, wc = gather_w[0], gather_w[len(gather_w) // 2], gather_w[-1]
-    for part in gather_c:
-        part.step2()
-    for part in gather_c:
-        part.step3()
-    wa.step2()
-    for part in gather_c:
-        part.step4()
-    if wb is not wa:
-        wb.step2()
-    for part in gather_c:
-        part.finish()
-    assemble(Gc, Wc, lay.rc, lay.jc, wide, thin_c)
+    gc.step2()
+    gc.step3()
+    gc.step4()
+    gd.step2()
+    gu.step2()
+    gc.step5()
+    gc.finish()
+    assemble(Gc, Wc, lay.rc, order_c, wide, thin_c)
 
     eye = (iota((16, 128), 0) == iota((16, 128), 1)).astype(F32).astype(BF16)
     rows_c = dot_nt(eye, Wc[:, (lay.bc + 2) * 128 : (lay.bc + 3) * 128])
@@ -594,10 +652,18 @@
             parts.append(jnp.concatenate([a, b], 0))
         return parts
 
-    GF = FWD_ROWS // 128
+    GF = lay.fwd_rows // 128
+
+    hook_f = hooks({
+            (0, 0): [gu.step3],
+            (1, 0): [gu.step4],
+            (1, 4): [gd.step3],
+            (3, 0): [gu.step5],
+            (3, 1): [gd.step4],
+        })
 
     def forward(i, _):
-        rows = pl.ds(pl.multiple_of(i * FWD_ROWS, FWD_ROWS), FWD_ROWS)
+        rows = pl.ds(pl.multiple_of(i * lay.fwd_rows, lay.fwd_rows), lay.fwd_rows)
         table = jnp.concatenate([Wc[:, lookup], table_low], 0)
         e = jnp.concatenate([dot_tn(h, table) for h in onehots(i, GF)], 0)
         xhat, scale1 = norm_stats(e)
@@ -606,6 +672,7 @@
         n1s[rows, :] = n1
         qkv = low(dot(n1, Wc[:, AQ]))
         qkvs[rows, :] = qkv
+        hook_f(i, 0)
         mixed = []
         for k in range(GF):
             visible = key_row < ints[pl.ds(32 + i * GF + k, 1), :].reshape(1, 1, 128)
@@ -624,6 +691,7 @@
             mixed.append(jnp.concatenate(pair_out, 1))
         o = low(jnp.concatenate(mixed, 0))
         os[rows, :] = o
+        hook_f(i, 1)
         r1 = e + dot(o, Wc[:, AO])
         xhat, scale2 = norm_stats(r1)
         n2 = low(xhat * gain2 + shift2)
@@ -631,12 +699,14 @@
         n2s[rows, :] = n2
         alphas[rows, 64:65] = scale1
         alphas[rows, 65:66] = scale2
+        hook_f(i, 2)
         value, slope = gelu_both(dot(n2, Wc[:, AU]))
         act = low(value)
         acts[rows, :] = act
         slopes[rows, :] = low(slope)
         r2 = low(r1 + dot_nt(act, Wc[:, AD]))
         r2s[rows, :] = r2
+        hook_f(i, 3)
         for k in range(GF):
             r = i * GF + k
             own = r2[k * 128 : (k + 1) * 128]
@@ -649,38 +719,32 @@
             u = dot_tn(low(alpha)[:, :32], own)
             for h in range(CH):
                 Us[h, pl.ds(pl.multiple_of(r * 8, 8), 8), :] = u[8 * h : 8 * h + 8]
+        hook_f(i, 4)
         return 0
 
-    events = {
-        0: [wc.step2, wa.step3],
-        2: [wb.step3],
-        3: [wa.step4],
-        4: [wc.step3],
-        5: [wb.step4],
-        7: [wc.step4],
-    }
-    lax.fori_loop(0, LEN * W // FWD_ROWS, with_events(forward, events), 0)
+    lax.fori_loop(0, LEN * W // lay.fwd_rows, forward, 0)
 
     head_c = [iota((1, C), 1) // HD == h for h in range(CH)]
     pooled = sum(jnp.where(head_c[h], dot(low(Us[h]), Wc[:, PV]), 0.0) for h in range(CH))
     pooled_low = low(pooled)
     w_in = dot(pooled_low, Wc[:, PR])
 
-    for part in gather_w:
-        part.finish()
+    gu.finish()
+    if lay.rw < 16:
+        gd.finish()
     if lay.rw >= 16:
 
         def wcols(lo, hi):
             return jnp.concatenate(
                 [
-                    Gw[:, :, :, :, j * lay.rw : (j + 1) * lay.rw, :].reshape(D, 128)
-                    for j in range(lo // 128, hi // 128)
+                    Gw[:, :, :, :, p * lay.rw : (p + 1) * lay.rw, :].reshape(D, 128)
+                    for p in [lay.word_at[j] for j in range(lo // 128, hi // 128)]
                 ],
                 1,
             )
 
     else:
-        assemble(Gw, Wwt, lay.rw, lay.jw, wide, thin_w)
+        assemble(Gw, Wwt, lay.rw, lay.word_order, wide, thin_w)
 
         def wcols(lo, hi):
             return Wwt[:, lo:hi]
@@ -712,10 +776,6 @@
     m2 = low(xhat2 * f2 + c2)
     value, slope = gelu_both(dot(m2, wcols(*BU)))
     aw = low(value)
-    out_y[...] = low(x + dot_nt(aw, wcols(*BD)))
-    outs = Outs(out_sem)
-    outs.start(out_y, y_out)
-
     ins[9].wait()
     gy = cot[...]
     dy = gy.astype(F32)
@@ -728,37 +788,52 @@
         for first in range(0, lay.jw, unit_w):
             ready = range(first, first + unit_w)
             if all(j in waiting for j in ready):
-                pack_blocks(PBw, first, [waiting.pop(j) for j in ready], rw, wide, thick)
-
-    cuts = [c * rw for c in lay.word_cuts]
-    nrecv = len(recv) // 5
+                some = [waiting.pop(j) for j in ready]
+                if rw >= 16 and first >= lay.word_cuts[2]:
+                    pack_blocks(PBd, first - lay.word_cuts[2], some, rw, wide, thick)
+                else:
+                    pack_blocks(Gw, first, some, rw, wide, thick)
+
     rs = Copies(rs_send, rs_recv)
-    scatters = [
-        Scatter(g, PBw, recv[6 * k : 6 * k + 6], rs, cuts[k], cuts[k + 1]) for k in range(3)
-    ]
+    land = list(recv)
+    first_d = 0 if rw >= 16 else cuts[2]
     cut1 = lay.j1 * lay.rc
-    scatters.append(Scatter(g, PBc, recv[18:24], rs, 0, cut1))
-    scatters.append(Scatter(g, PBc, recv[24:30], rs, cut1, PBc.shape[4]))
-    w1, w2, w3, c1_, c2_ = scatters
-    if lay.rw < 16:
-        for part in gather_w:
-            part.drain()
+    w1 = scatter_pair(g, PBd if rw >= 16 else Gw, land, rs, first_d, first_d + cuts[3] - cuts[2])
+    w2 = scatter_pair(g, Gw, land, rs, cuts[1], cuts[2])
+    w3 = scatter_pair(g, Gw, land, rs, 0, cuts[1])
+    s1 = scatter_pair(g, Gc, land, rs, 0, cut1)
+    s2 = scatter_pair(g, Gc, land, rs, cut1, Gc.shape[4])
+    if rw < 16:
+        gu.drain()
+        gd.drain()
+    at = lay.word_cuts[2]
+    gd.step5()
     for k in range(0, FF, 512):
-        put_w(k // 128, columns(dot_tn(gy, aw[:, k : k + 512])))
-    w1.start()
+        put_w(at + k // 128, columns(dot_tn(gy, aw[:, k : k + 512])))
+    w1.step1()
+    pass
+    if rw >= 16:
+        gd.finish()
+        gu.drain()
+        gd.drain()
+    out_y[...] = low(x + dot_nt(aw, wcols(*BD)))
+    outs = Outs(out_sem)
+    outs.start(out_y, y_out)
     gzw = low(slope * dot(gy, wcols(*BD)))
+    pass
+    dm2 = dot_nt(gzw, wcols(*BU))
+    at = lay.word_cuts[1]
     for k in range(0, FF, 512):
-        put_w((FF + k) // 128, columns(dot_tn(m2, gzw[:, k : k + 512])))
-    w2.start()
+        put_w(at + k // 128, columns(dot_tn(m2, gzw[:, k : k + 512])))
+    w2.step1()
     w1.step2()
-    dm2 = dot_nt(gzw, wcols(*BU))
     gf2 = jnp.sum(dm2 * xhat2, 0, keepdims=True)
     gc2 = jnp.sum(dm2, 0, keepdims=True)
     dx = dy + norm_back(dm2, xhat2, sc2, f2)
     gx = low(dx)
-    put_w((2 * FF + BO[0]) // 128, columns(dot_tn(ow, gx)))
     gow = low(dot_nt(gx, wcols(*BO)))
-    w2.step2()
+    put_w(BO[0] // 128, columns(dot_tn(ow, gx)))
+    pass
     gq, gk, gv = [], [], []
     for p in range(NP):
         go = gow[:, p * 128 : (p + 1) * 128]
@@ -769,34 +844,37 @@
         gk.append(dot(side_by_side(gs, 128), qst[p]) * 0.125)
         gv.append(dot(side_by_side(low(pw[p]).reshape(256, 128), 128), head_stack(go, heads)))
     tg = low(jnp.concatenate(gq + gk + gv, 1))
+    dm1 = dot_nt(tg, wcols(*BQ))
     for k in range(0, 3 * D, 512):
-        put_w((2 * FF + k) // 128, columns(dot_tn(m1, tg[:, k : k + 512])))
-    dm1 = dot_nt(tg, wcols(*BQ))
+        put_w(k // 128, columns(dot_tn(m1, tg[:, k : k + 512])))
     gf1 = jnp.sum(dm1 * xhat1, 0, keepdims=True)
     gc1 = jnp.sum(dm1, 0, keepdims=True)
     dw = dx + norm_back(dm1, xhat1, sc1, f1)
     vec_rows = low(jnp.concatenate([gf1, gc1, gf2, gc2, jnp.zeros((12, D), F32)], 0))
-    zero_w = [jnp.zeros((D, 128), F32)] * (lay.jw - lay.bw - 1)
-    put_w(lay.bw, [dot_tn(vec_rows, eye)] + zero_w)
-    w3.start()
-
-    for part in gather_c:
-        part.drain()
+    at = lay.word_at[lay.bw]
+    put_w(at, [dot_tn(vec_rows, eye)] + [jnp.zeros((D, 128), F32)] * (lay.word_cuts[1] - at - 1))
+    w3.step1()
+    w2.step2()
+
+    gc.drain()
     gw = low(dw)
     dpool = dot_nt(gw, Wc[:, PR])
+    pass
     dp4 = jnp.concatenate([low(jnp.where(head_c[h], dpool, 0.0)) for h in range(CH)], 0)
     Ys[...] = dot_nt(dp4, Wc[:, PV]).reshape(CH, LEN, C)
     for ref in (accq, acco, accu, accd, acct, sums, tsum):
         ref[...] = jnp.zeros(ref.shape, F32)
 
     map32 = map_hi[:32]
-    GB = BWD_ROWS // 128
+    GB = lay.bwd_rows // 128
+
+    GP = lay.ffn_rows // 128
 
     def back_ffn(i, _):
-        rows = pl.ds(pl.multiple_of(i * BWD_ROWS, BWD_ROWS), BWD_ROWS)
+        rows = pl.ds(pl.multiple_of(i * lay.ffn_rows, lay.ffn_rows), lay.ffn_rows)
         parts = []
-        for k in range(GB):
-            r = i * GB + k
+        for k in range(GP):
+            r = i * GP + k
             own = r2s[pl.ds(pl.multiple_of(r * 128, 128), 128), :]
             alpha = alphas[pl.ds(pl.multiple_of(r * 128, 128), 128), 0:32]
             yg = low(
@@ -810,18 +888,24 @@
             parts.append(dot(low(alpha), yg) + dot(dr, map32))
         dr2 = jnp.concatenate(parts, 0)
         g2 = low(dr2)
+        hook_1(i, 0)
         accd[...] += dot_tn(g2, acts[rows, :])
+        hook_1(i, 1)
         gz = low(slopes[rows, :].astype(F32) * dot(g2, Wc[:, AD]))
         accu[...] += dot_tn(n2s[rows, :], gz)
+        hook_1(i, 2)
         dn = dot_nt(gz, Wc[:, AU])
         xhat = xh2[rows, :].astype(F32)
         sums[2:3, :] += jnp.sum(dn * xhat, 0, keepdims=True)
         sums[3:4, :] += jnp.sum(dn, 0, keepdims=True)
         dr1s[rows, :] = dr2 + norm_back(dn, xhat, alphas[rows, 65:66], gain2)
+        hook_1(i, 3)
         return 0
 
     def place_w(j, value):
         j = lay.word_order[j]
+        if j is None:
+            return
         if j < lay.bw:
             put(out_wm, lay.bw, j, value)
         else:
@@ -843,21 +927,26 @@
             out_group[...] = value[:, 0:LANGS]
             out_vec[...] = value[:, LANGS : LANGS + 5]
 
-    def fin_w(k):
-        first = lay.word_cuts[k]
-        count = min(lay.word_cuts[k + 1], lay.bw + 1) - first
-        return lambda: scatters[k].finish(lambda j, v: place_w(first + j, v), rw, count)
-
-    nb = LEN * W // BWD_ROWS
-    events = {
-        0: [w3.step2],
-        1: [w1.step3],
-        3: [w2.step3],
-        4: [w1.step4],
-        6: [w3.step3],
-        7: [w2.step4],
-    }
-    lax.fori_loop(0, nb, with_events(back_ffn, events), 0)
+    def fin_w1():
+        w1.finish(lambda j, v: place_w(lay.word_cuts[2] + j, v), rw, first_d, FF // 128)
+
+    def fin_w2():
+        w2.finish(lambda j, v: place_w(lay.word_cuts[1] + j, v), rw, cuts[1], FF // 128)
+
+    def fin_w3():
+        w3.finish(place_w, rw, 0, lay.word_cuts[1])
+
+    def fin_s1():
+        s1.finish(place_1, rc, 0, 24)
+
+    def fin_s2():
+        s2.finish(place_2, rc, cut1, 11)
+
+    hook_1 = hooks({
+            (0, 3): [w1.step3, w3.step2],
+            (3, 2): [w1.step4, w2.step3],
+        })
+    lax.fori_loop(0, LEN * W // lay.ffn_rows, back_ffn, 0)
 
     grad_pr = dot_tn(pooled_low, gw)
     grad_pv = dot_tn(low(Us[...]).reshape(CH * LEN, C), dp4)
@@ -874,18 +963,20 @@
         wide,
         thick,
     )
-    c1_.start()
+    s1.step1()
+    pass
     gpq = dot(t_low, Wc[:, PK]) * 0.125
     gpq = jnp.sum(
         jnp.where(iota((32, C), 0) // 8 == iota((32, C), 1) // HD, gpq, 0.0), 0, keepdims=True
     )
 
     def back_attention(i, _):
-        rows = pl.ds(pl.multiple_of(i * BWD_ROWS, BWD_ROWS), BWD_ROWS)
+        rows = pl.ds(pl.multiple_of(i * lay.bwd_rows, lay.bwd_rows), lay.bwd_rows)
         dr1 = dr1s[rows, :]
         g1 = low(dr1)
         acco[...] += dot_tn(os[rows, :], g1)
         go = low(dot_nt(g1, Wc[:, AO]))
+        hook_2(i, 0)
         qkv = qkvs[rows, :]
         grads = [[], [], []]
         for k in range(GB):
@@ -906,25 +997,29 @@
                 part[2].append(dot(side_by_side(pb, 128), head_stack(gop, heads)))
             for b in range(3):
                 grads[b].append(jnp.concatenate(part[b], 1))
+        hook_2(i, 1)
         tg = low(jnp.concatenate([jnp.concatenate(b, 0) for b in grads], 1))
         accq[...] += dot_tn(n1s[rows, :], tg)
         dn = dot_nt(tg, Wc[:, AQ])
+        hook_2(i, 2)
         xhat = xh1[rows, :].astype(F32)
         sums[0:1, :] += jnp.sum(dn * xhat, 0, keepdims=True)
         sums[1:2, :] += jnp.sum(dn, 0, keepdims=True)
         ge = low(dr1 + norm_back(dn, xhat, alphas[rows, 64:65], gain1))
         for k, h in enumerate(onehots(i, GB)):
             acct[...] += dot(h, ge[k * 128 : (k + 1) * 128])
+        hook_2(i, 3)
         return 0
 
-    events = {
-        1: [c1_.step2, fin_w(0)],
-        2: [w3.step4],
-        4: [c1_.step3, fin_w(1)],
-        6: [c1_.step4],
-    }
-    lax.fori_loop(0, nb, with_events(back_attention, events), 0)
-
+    hook_2 = hooks({
+            (0, 2): [w3.step3],
+            (1, 0): [w2.step4, s1.step2],
+            (2, 2): [w3.step4],
+            (3, 2): [s1.step3],
+        })
+    lax.fori_loop(0, LEN * W // lay.bwd_rows, back_attention, 0)
+
+    pass
     small = low(jnp.concatenate([acct[VOCAB : VOCAB + 8], sums[0:4], gpq, jnp.zeros((3, C), F32)], 0))
     pad2 = [jnp.zeros((C, 128), F32)] * (lay.j2 - 11)
     pack_blocks(
@@ -936,20 +1031,23 @@
         wide,
         thick,
     )
-    c2_.start()
-    fin_w(2)()
+    s2.step1()
+    s2.step2()
+    s1.step4()
+    s2.step3()
+    fin_w2()
+    fin_w1()
+    s2.step4()
+    fin_w3()
     outs.start(out_wm, wm_out)
     outs.start(out_wvec, wvec_out)
-    c2_.step2()
-    c1_.finish(place_1, rc, 24)
-    c2_.step3()
-    c2_.step4()
-    c2_.finish(place_2, rc, 11)
+    fin_s1()
+    fin_s2()
     outs.start(out_cm, cm_out)
     outs.start(out_lookup, lookup_out)
     outs.start(out_group, group_out)
     outs.start(out_vec, vec_out)
-    for part in (gather_w if lay.rw >= 16 else []) + scatters:
+    for part in (w1, w2, w3, s1, s2):
         part.drain()
     outs.wait()
 
@@ -986,10 +1084,9 @@
     Y, Z, X = sizes
     rows = LEN * W
     rows_c, rows_w = lay.jc * lay.rc, lay.jw * lay.rw
-    rows_1, rows_2 = lay.j1 * lay.rc, lay.j2 * lay.rc
-    word_parts = [(b - a) * lay.rw for a, b in zip(lay.word_cuts, lay.word_cuts[1:])]
-    nag = ag_count(Y, Z, X) * (AG_PARTS_C + AG_PARTS_W)
-    nrs = rs_count(Y, Z, X) * 5
+    rows_1 = lay.j1 * lay.rc
+    nag = ag_count(Y, Z, X) * 6
+    nrs = rs_count(Y, Z, X) * 10
     dma = pltpu.SemaphoreType.DMA
 
     def vm(shape, dtype):
@@ -1028,9 +1125,9 @@
         vm((64, 128), jnp.int32),
         vm(lay.lead + (rows_c, 128), BF16),
         vm(lay.lead + (rows_w, 128), BF16),
+        vm(lay.lead + (FF // 128 * lay.rw, 128) if lay.rw >= 16 else (16, 128), BF16),
         vm((C, (lay.bc + 3) * 128), BF16),
         vm((D, (lay.bw + 1) * 128) if lay.rw < 16 else (16, 128), BF16),
-        vm(lay.lead + (rows_w, 128) if lay.rw >= 16 else (16, 128), BF16),
         like(outs[1]),
         like(outs[5]),
         vm((rows, C), BF16),
@@ -1065,8 +1162,9 @@
         dma((nrs,)),
         dma((nrs,)),
     ]
-    for n in word_parts + [rows_1, rows_2]:
-        scratch += rs_scratch(Y, Z, X, n)
+    at = [c * lay.rw for c in lay.word_cuts]
+    for lo, hi in ((at[2], at[3]), (at[1], at[2]), (at[0], at[1]), (0, rows_1), (rows_1, rows_c)):
+        scratch += scatter_pair_scratch(sizes, lo, hi)
     anywhere = pl.BlockSpec(memory_space=pl.ANY)
     in_specs = [anywhere] * 11
     in_specs[3] = pl.BlockSpec(memory_space=pltpu.SMEM)

time: 128 us -> 116 us (0.906)
  Pallas kernels: 127 us -> 114 us
    pallas_call x1, Pallas kernels: 125 us -> 112 us  [shards(): pl.pallas_call(functools.partial(mono, lay, STAGE), out_shape=outs, in_sp...]
where the time goes in v2:
time: 116 us
  Pallas kernels  114 us (98%)
  between operations  1.45 us (1%)
    pallas_call x1, Pallas kernels, shards(): pl.pallas_call(functools.partial(mono, lay, STAGE), out_shape=outs, in_sp...  112 us

profile of v2, /device:TPU:0, one launch (start us, length us, event | category | flops | bytes accessed | tf_op | source)
XLA Modules:
  0.0 115.5 jit_solution(2284191373522568090)
XLA Ops:
  1.3 112.0 %layer.1 = (bf16[128,512]{1,0:T(8,128)(2,1)}, f32[256,128]{1,0:T(8,128)}, f32[8,256]{1,0:T(8,128)}, f32[8,8]{1,0:T(8,128)}, f32[8,5]{1,0:T(8,128)}, /*index=5*/f32[768,128]{1,0:T(8,128)}, f32[4,16]{1,0:T(4,128)}) custom-call(s32[16,128]{1,0:T(8,128)} %bitcast.8, s32[1,128]{1,0:T(1,128)} %counts_in.1, s32[1,128]{1,0:T(1,128)} %langs_in.1, s32[1]{0:T(128)S(6)} %copy.18.length, ...), custom_call_target="tpu_custom_call" | custom-call | tf_op jit(solution)/shard_map/layer/pallas_call | solution.py:1171
  113.3 2.0 %hand_over.1 = (bf16[128,512]{1,0:T(8,128)(2,1)}, f32[256,128]{1,0:T(8,128)}, f32[8,256]{1,0:T(8,128)}, f32[8,8]{1,0:T(8,128)}, f32[8,5]{1,0:T(8,128)}, /*index=5*/f32[768,128]{1,0:T(8,128)}, f32[4,16]{1,0:T(4,128)}) custom-call(bf16[128,512]{1,0:T(8,128)(2,1)} %get-tuple-element.21.refs_0_, f32[256,128]{1,0:T(8,128)} %get-tuple-element.22.refs_1_, ...), custom_call_target="tpu_custom_call" | custom-call | tf_op jit(solution)/shard_map/hand_over/pallas_call | solution.py:1182

commit v3 on v2

--- a/solution.py
+++ b/solution.py
@@ -24,9 +24,9 @@
 NEGATIVE = -1000000000.0
 F32 = jnp.float32
 BF16 = jnp.bfloat16
-FWD_ROWS = 512
-BWD_ROWS = 512
-FFN_ROWS = 512
+FWD_ROWS = 1024
+BWD_ROWS = 1024
+FFN_ROWS = 1024
 VMEM_LIMIT = 63 << 20
 STAGE = 0
 
@@ -187,20 +187,25 @@
     total = 1
     for n in lead:
         total *= n
+    some = next(n for n in (16, 8, 4, 2, 1) if total % n == 0)
 
     def body(i, _):
-        idx, r = [], i
-        for n in reversed(lead):
-            idx.append(r % n)
-            r = r // n
-        idx = tuple(reversed(idx))
-        acc = dst[idx].astype(F32)
-        for s in srcs:
-            acc = acc + s[idx].astype(F32)
-        dst[idx] = acc.astype(BF16)
+        for part in range(some):
+            idx, r = [], i * some + part
+            for n in reversed(lead):
+                idx.append(r % n)
+                r = r // n
+            idx = tuple(reversed(idx))
+            if len(srcs) == 1:
+                dst[idx] = dst[idx] + srcs[0][idx]
+                continue
+            acc = dst[idx].astype(F32)
+            for s in srcs:
+                acc = acc + s[idx].astype(F32)
+            dst[idx] = acc.astype(BF16)
         return 0
 
-    lax.fori_loop(0, total, body, 0)
+    lax.fori_loop(0, total // some, body, 0)
 
 
 class Scatter:
@@ -488,7 +493,7 @@
             return max(-(-n // unit), 2) * unit
 
         self.jc = padded(self.bc + 3, self.rc)
-        self.j1 = padded(24, self.rc)
+        self.j1 = padded(26, self.rc)
         self.j2 = self.jc - self.j1
         thin = self.rc < 8
         self.fwd_rows = 256 if thin else FWD_ROWS
@@ -564,7 +569,7 @@
     out_y, out_lookup, out_group, out_vec, out_wvec, exc, exw, ints,
     Gc, Gw, PBd, Wc, Wwt, out_cm, out_wm,
     xh1, n1s, qkvs, probs, os, xh2, n2s, acts, slopes, r2s, alphas, dr1s,
-    Us, Ys, accq, acco, accu, accd, acct, sums, tsum,
+    Us, Ys, acct, sums, tsum,
     wide, thin_c, thin_w, thick,
     in_sem, out_sem, ag_send, ag_recv, rs_send, rs_recv, *recv,
 ):
@@ -611,10 +616,11 @@
     gc.step2()
     gc.step3()
     gc.step4()
-    gd.step2()
     gu.step2()
     gc.step5()
     gc.finish()
+    gu.step3()
+    gd.step2()
     assemble(Gc, Wc, lay.rc, order_c, wide, thin_c)
 
     eye = (iota((16, 128), 0) == iota((16, 128), 1)).astype(F32).astype(BF16)
@@ -655,11 +661,9 @@
     GF = lay.fwd_rows // 128
 
     hook_f = hooks({
-            (0, 0): [gu.step3],
-            (1, 0): [gu.step4],
-            (1, 4): [gd.step3],
-            (3, 0): [gu.step5],
-            (3, 1): [gd.step4],
+            (0, 2): [gu.step4],
+            (0, 4): [gd.step3],
+            (1, 3): [gu.step5, gd.step4],
         })
 
     def forward(i, _):
@@ -807,11 +811,12 @@
         gu.drain()
         gd.drain()
     at = lay.word_cuts[2]
-    gd.step5()
+    pass
     for k in range(0, FF, 512):
         put_w(at + k // 128, columns(dot_tn(gy, aw[:, k : k + 512])))
     w1.step1()
-    pass
+    gd.step5()
+    w1.step2()
     if rw >= 16:
         gd.finish()
         gu.drain()
@@ -826,7 +831,7 @@
     for k in range(0, FF, 512):
         put_w(at + k // 128, columns(dot_tn(m2, gzw[:, k : k + 512])))
     w2.step1()
-    w1.step2()
+    pass
     gf2 = jnp.sum(dm2 * xhat2, 0, keepdims=True)
     gc2 = jnp.sum(dm2, 0, keepdims=True)
     dx = dy + norm_back(dm2, xhat2, sc2, f2)
@@ -862,7 +867,7 @@
     pass
     dp4 = jnp.concatenate([low(jnp.where(head_c[h], dpool, 0.0)) for h in range(CH)], 0)
     Ys[...] = dot_nt(dp4, Wc[:, PV]).reshape(CH, LEN, C)
-    for ref in (accq, acco, accu, accd, acct, sums, tsum):
+    for ref in (acct, sums, tsum):
         ref[...] = jnp.zeros(ref.shape, F32)
 
     map32 = map_hi[:32]
@@ -889,16 +894,18 @@
         dr2 = jnp.concatenate(parts, 0)
         g2 = low(dr2)
         hook_1(i, 0)
-        accd[...] += dot_tn(g2, acts[rows, :])
+        r2s[rows, :] = g2
         hook_1(i, 1)
         gz = low(slopes[rows, :].astype(F32) * dot(g2, Wc[:, AD]))
-        accu[...] += dot_tn(n2s[rows, :], gz)
+        slopes[rows, :] = gz
         hook_1(i, 2)
         dn = dot_nt(gz, Wc[:, AU])
         xhat = xh2[rows, :].astype(F32)
         sums[2:3, :] += jnp.sum(dn * xhat, 0, keepdims=True)
         sums[3:4, :] += jnp.sum(dn, 0, keepdims=True)
-        dr1s[rows, :] = dr2 + norm_back(dn, xhat, alphas[rows, 65:66], gain2)
+        dr1 = dr2 + norm_back(dn, xhat, alphas[rows, 65:66], gain2)
+        dr1s[rows, :] = dr1
+        xh2[rows, :] = low(dr1)
         hook_1(i, 3)
         return 0
 
@@ -916,13 +923,13 @@
             )[0:4]
 
     def place_1(j, value):
-        put(out_cm, lay.bc, 8 + j, value)
+        put(out_cm, lay.bc, 8 + j if j < 24 else j - 18, value)
 
     def place_2(j, value):
-        if j < 8:
+        if j < 6:
             put(out_cm, lay.bc, j, value)
-        elif j < 10:
-            out_lookup[:, (j - 8) * 128 : (j - 7) * 128] = value
+        elif j < 8:
+            out_lookup[:, (j - 6) * 128 : (j - 5) * 128] = value
         else:
             out_group[...] = value[:, 0:LANGS]
             out_vec[...] = value[:, LANGS : LANGS + 5]
@@ -937,14 +944,13 @@
         w3.finish(place_w, rw, 0, lay.word_cuts[1])
 
     def fin_s1():
-        s1.finish(place_1, rc, 0, 24)
+        s1.finish(place_1, rc, 0, 26)
 
     def fin_s2():
-        s2.finish(place_2, rc, cut1, 11)
+        s2.finish(place_2, rc, cut1, 9)
 
     hook_1 = hooks({
-            (0, 3): [w1.step3, w3.step2],
-            (3, 2): [w1.step4, w2.step3],
+            (1, 0): [w1.step3, w3.step2],
         })
     lax.fori_loop(0, LEN * W // lay.ffn_rows, back_ffn, 0)
 
@@ -953,18 +959,19 @@
     t_low = low(tsum[...])
     grad_pk = dot_tn(t_low, low(pq_rows[:32]))
     rc = lay.rc
-    pad1 = [jnp.zeros((C, 128), F32)] * (lay.j1 - 24)
+    pad1 = [jnp.zeros((C, 128), F32)] * (lay.j1 - 26)
     pack_blocks(
         PBc,
         0,
-        columns(accu[...]) + columns(accd[...]) + columns(grad_pk) + columns(grad_pv)
-        + columns(grad_pr) + pad1,
+        columns(dot_tn(n2s[...], slopes[...])) + columns(dot_tn(r2s[...], acts[...])) + columns(grad_pk) + columns(grad_pv)
+        + columns(grad_pr) + columns(dot_tn(os[...], xh2[...])) + pad1,
         rc,
         wide,
         thick,
     )
     s1.step1()
-    pass
+    w1.step4()
+    w2.step3()
     gpq = dot(t_low, Wc[:, PK]) * 0.125
     gpq = jnp.sum(
         jnp.where(iota((32, C), 0) // 8 == iota((32, C), 1) // HD, gpq, 0.0), 0, keepdims=True
@@ -973,9 +980,7 @@
     def back_attention(i, _):
         rows = pl.ds(pl.multiple_of(i * lay.bwd_rows, lay.bwd_rows), lay.bwd_rows)
         dr1 = dr1s[rows, :]
-        g1 = low(dr1)
-        acco[...] += dot_tn(os[rows, :], g1)
-        go = low(dot_nt(g1, Wc[:, AO]))
+        go = low(dot_nt(xh2[rows, :], Wc[:, AO]))
         hook_2(i, 0)
         qkv = qkvs[rows, :]
         grads = [[], [], []]
@@ -999,46 +1004,45 @@
                 grads[b].append(jnp.concatenate(part[b], 1))
         hook_2(i, 1)
         tg = low(jnp.concatenate([jnp.concatenate(b, 0) for b in grads], 1))
-        accq[...] += dot_tn(n1s[rows, :], tg)
+        qkvs[rows, :] = tg
         dn = dot_nt(tg, Wc[:, AQ])
         hook_2(i, 2)
         xhat = xh1[rows, :].astype(F32)
         sums[0:1, :] += jnp.sum(dn * xhat, 0, keepdims=True)
         sums[1:2, :] += jnp.sum(dn, 0, keepdims=True)
         ge = low(dr1 + norm_back(dn, xhat, alphas[rows, 64:65], gain1))
-        for k, h in enumerate(onehots(i, GB)):
-            acct[...] += dot(h, ge[k * 128 : (k + 1) * 128])
+        acct[...] += dot(jnp.concatenate(onehots(i, GB), 1), ge)
         hook_2(i, 3)
         return 0
 
     hook_2 = hooks({
             (0, 2): [w3.step3],
-            (1, 0): [w2.step4, s1.step2],
-            (2, 2): [w3.step4],
-            (3, 2): [s1.step3],
+            (0, 3): [s1.step2, w2.step4],
         })
     lax.fori_loop(0, LEN * W // lay.bwd_rows, back_attention, 0)
 
     pass
     small = low(jnp.concatenate([acct[VOCAB : VOCAB + 8], sums[0:4], gpq, jnp.zeros((3, C), F32)], 0))
-    pad2 = [jnp.zeros((C, 128), F32)] * (lay.j2 - 11)
+    pad2 = [jnp.zeros((C, 128), F32)] * (lay.j2 - 9)
     pack_blocks(
         PBc,
         lay.j1,
-        columns(accq[...]) + columns(acco[...]) + columns(acct[0:VOCAB, :])
+        columns(dot_tn(n1s[...], qkvs[...])) + columns(acct[0:VOCAB, :])
         + [dot_tn(small, eye)] + pad2,
         rc,
         wide,
         thick,
     )
     s2.step1()
+    w3.step4()
+    s1.step3()
+    fin_w1()
     s2.step2()
     s1.step4()
     s2.step3()
-    fin_w2()
-    fin_w1()
     s2.step4()
     fin_w3()
+    fin_w2()
     outs.start(out_wm, wm_out)
     outs.start(out_wvec, wvec_out)
     fin_s1()
@@ -1144,10 +1148,6 @@
         vm((rows, C), F32),
         vm((CH, LEN, C), F32),
         vm((CH, LEN, C), F32),
-        vm((C, 3 * C), F32),
-        vm((C, C), F32),
-        vm((C, CM), F32),
-        vm((C, CM), F32),
         vm((VOCAB + 16, C), F32),
         vm((8, C), F32),
         vm((32, C), F32),

time: 116 us -> 110 us (0.948)
  Pallas kernels: 114 us -> 108 us
    pallas_call x1, Pallas kernels: 112 us -> 106 us  [shards(): pl.pallas_call(functools.partial(mono, lay, STAGE), out_shape=outs, in_sp...]
where the time goes in v3:
time: 110 us
  Pallas kernels  108 us (98%)
  between operations  1.47 us (1%)
    pallas_call x1, Pallas kernels, shards(): pl.pallas_call(functools.partial(mono, lay, STAGE), out_shape=outs, in_sp...  106 us

profile of v3, /device:TPU:0, one launch (start us, length us, event | category | flops | bytes accessed | tf_op | source)
XLA Modules:
  0.0 109.9 jit_solution(16490873321999395652)
XLA Ops:
  1.3 106.4 %layer.1 = (bf16[128,512]{1,0:T(8,128)(2,1)}, f32[256,128]{1,0:T(8,128)}, f32[8,256]{1,0:T(8,128)}, f32[8,8]{1,0:T(8,128)}, f32[8,5]{1,0:T(8,128)}, /*index=5*/f32[768,128]{1,0:T(8,128)}, f32[4,16]{1,0:T(4,128)}) custom-call(s32[16,128]{1,0:T(8,128)} %bitcast.8, s32[1,128]{1,0:T(1,128)} %counts_in.1, s32[1,128]{1,0:T(1,128)} %langs_in.1, s32[1]{0:T(128)S(6)} %copy.18.length, ...), custom_call_target="tpu_custom_call" | custom-call | tf_op jit(solution)/shard_map/layer/pallas_call | solution.py:1171
  107.7 2.0 %hand_over.1 = (bf16[128,512]{1,0:T(8,128)(2,1)}, f32[256,128]{1,0:T(8,128)}, f32[8,256]{1,0:T(8,128)}, f32[8,8]{1,0:T(8,128)}, f32[8,5]{1,0:T(8,128)}, /*index=5*/f32[768,128]{1,0:T(8,128)}, f32[4,16]{1,0:T(4,128)}) custom-call(bf16[128,512]{1,0:T(8,128)(2,1)} %get-tuple-element.21.refs_0_, f32[256,128]{1,0:T(8,128)} %get-tuple-element.22.refs_1_, ...), custom_call_target="tpu_custom_call" | custom-call | tf_op jit(solution)/shard_map/hand_over/pallas_call | solution.py:1182

commit v4 on v3

--- a/solution.py
+++ b/solution.py
@@ -169,7 +169,7 @@
 
 
 def rs_count(Y, Z, X):
-    return 1 + (Z - 1) + (X - 1) + (Y - 1)
+    return 1 + (Z - 1) + ((X - 1) + (Y - 1)) * Z
 
 
 def rs_scratch(sizes, rows, order):
@@ -214,55 +214,69 @@
         self.lo, self.hi = lo, hi
         first = len(copies.made)
         rows = slice(lo, hi)
+        one, two, three = order
         me = {"y": g.y, "z": g.z, "x": g.x}
-        have = {"y": ALL, "z": ALL, "x": ALL}
+        own = {axis: pl.ds(v, 1) for axis, v in me.items()}
 
         def slot(c, **at):
-            v = {**have, **at}
+            v = {"y": ALL, "z": ALL, "x": ALL, **at}
             return (v["y"], c, v["z"], v["x"], rows)
 
-        self.hops = [[copies.plan(PB.at[slot(1 - g.c)], recv[0], g.to_c)]]
-        self.sums = [PB.at[slot(g.c)]]
-        for n, axis in enumerate(order):
-            self.hops.append(
-                [
-                    copies.plan(PB.at[slot(g.c, **{axis: pl.ds(v, 1)})], recv[n + 1].at[k], to)
-                    for k, (v, to) in enumerate(zip(g.off[axis], g.to[axis]))
-                ]
-            )
-            have[axis] = pl.ds(me[axis], 1)
-            self.sums.append(PB.at[slot(g.c)])
+        def land(n, k, v):
+            at = {"y": ALL, "z": ALL, "x": ALL, three: pl.ds(v, 1)}
+            return recv[n].at[k, at["y"], at["z"], at["x"]]
+
+        def hop(n, axis, v, **at):
+            return [
+                copies.plan(PB.at[slot(g.c, **{**at, axis: pl.ds(u, 1), three: pl.ds(v, 1)})], land(n, k, v), to)
+                for k, (u, to) in enumerate(zip(g.off[axis], g.to[axis]))
+            ]
+
+        self.core = [copies.plan(PB.at[slot(1 - g.c)], recv[0], g.to_c)]
+        self.places = g.off[three] + [me[three]]
+        self.hop1 = [hop(1, one, v) for v in self.places]
+        self.hop2 = [hop(2, two, v, **{one: own[one]}) for v in self.places]
+        self.hop3 = [
+            copies.plan(PB.at[slot(g.c, **{**own, three: pl.ds(v, 1)})], recv[3].at[k], to)
+            for k, (v, to) in enumerate(zip(g.off[three], g.to[three]))
+        ]
+        self.sum0 = PB.at[slot(g.c)]
+        self.sum1 = [PB.at[slot(g.c, **{one: own[one], three: pl.ds(v, 1)})] for v in self.places]
+        self.sum2 = [PB.at[slot(g.c, **{**own, three: pl.ds(v, 1)})] for v in self.places]
+        self.from1 = [[land(1, k, v) for k in range(len(g.off[one]))] for v in self.places]
+        self.from2 = [[land(2, k, v) for k in range(len(g.off[two]))] for v in self.places]
         self.mine = range(first, len(copies.made))
 
-    def add(self, n):
-        self.copies.arrived(self.hops[n])
-        if n == 0:
-            add_into(self.sums[0], [self.recv[0]])
-        else:
-            add_into(self.sums[n], [self.recv[n].at[k] for k in range(len(self.hops[n]))])
-
     def step1(self):
-        self.copies.start(self.hops[0])
+        self.copies.start(self.core)
 
     def step2(self):
-        self.add(0)
-        self.copies.start(self.hops[1])
+        self.copies.arrived(self.core)
+        add_into(self.sum0, [self.recv[0]])
+        for which in self.hop1:
+            self.copies.start(which)
 
     def step3(self):
-        self.add(1)
-        self.copies.start(self.hops[2])
+        for k, which in enumerate(self.hop1):
+            self.copies.arrived(which)
+            add_into(self.sum1[k], self.from1[k])
+            self.copies.start(self.hop2[k])
 
     def step4(self):
-        self.add(2)
-        self.copies.start(self.hops[3])
+        for k, which in enumerate(self.hop2[:-1]):
+            self.copies.arrived(which)
+            add_into(self.sum2[k], self.from2[k])
+            self.copies.start(self.hop3[k : k + 1])
 
     def finish(self, place, rows, base, count):
-        self.copies.arrived(self.hops[3])
+        self.copies.arrived(self.hop2[-1] + self.hop3)
         size = max(rows, 16)
         for row in range(self.lo, self.hi, size):
             r = slice(row - self.lo, row - self.lo + size)
             acc = self.PB[self.g.me + (slice(row, row + size),)].astype(F32)
-            for k in range(len(self.hops[3])):
+            for part in self.from2[-1]:
+                acc = acc + part[0, 0, 0, r].astype(F32)
+            for k in range(len(self.hop3)):
                 acc = acc + self.recv[3][k, 0, 0, 0, r].astype(F32)
             for u in range(size // rows):
                 j = (row - base) // rows + u

time: 110 us -> 110 us (level)
  no operation moved by 1% of the time
where the time goes in v4:
time: 110 us
  Pallas kernels  109 us (99%)
  between operations  1.47 us (1%)
    pallas_call x1, Pallas kernels, shards(): pl.pallas_call(functools.partial(mono, lay, STAGE), out_shape=outs, in_sp...  107 us

profile of v4, /device:TPU:0, one launch (start us, length us, event | category | flops | bytes accessed | tf_op | source)
XLA Modules:
  0.0 110.0 jit_solution(11788531360007256831)
XLA Ops:
  1.3 106.5 %layer.1 = (bf16[128,512]{1,0:T(8,128)(2,1)}, f32[256,128]{1,0:T(8,128)}, f32[8,256]{1,0:T(8,128)}, f32[8,8]{1,0:T(8,128)}, f32[8,5]{1,0:T(8,128)}, /*index=5*/f32[768,128]{1,0:T(8,128)}, f32[4,16]{1,0:T(4,128)}) custom-call(s32[16,128]{1,0:T(8,128)} %bitcast.8, s32[1,128]{1,0:T(1,128)} %counts_in.1, s32[1,128]{1,0:T(1,128)} %langs_in.1, s32[1]{0:T(128)S(6)} %copy.18.length, ...), custom_call_target="tpu_custom_call" | custom-call | tf_op jit(solution)/shard_map/layer/pallas_call | solution.py:1185
  107.8 2.0 %hand_over.1 = (bf16[128,512]{1,0:T(8,128)(2,1)}, f32[256,128]{1,0:T(8,128)}, f32[8,256]{1,0:T(8,128)}, f32[8,8]{1,0:T(8,128)}, f32[8,5]{1,0:T(8,128)}, /*index=5*/f32[768,128]{1,0:T(8,128)}, f32[4,16]{1,0:T(4,128)}) custom-call(bf16[128,512]{1,0:T(8,128)(2,1)} %get-tuple-element.21.refs_0_, f32[256,128]{1,0:T(8,128)} %get-tuple-element.22.refs_1_, ...), custom_call_target="tpu_custom_call" | custom-call | tf_op jit(solution)/shard_map/hand_over/pallas_call | solution.py:1196
